TPU v7x, 256 devices: a whole 4x4x8 slice. The times are simulated.
256 devices in a mesh: grp: 32 (over y, z), tpl: 8 (over x, core).
Axes of the slice: x: 4, y: 4, z: 8, core: 2. Of those that a mesh axis runs over, the one named last changes fastest.
Arguments:
- strain: bfloat16 [512, 2, 262144], P('grp', None, 'tpl'), may hold values from -6 to 6
- templates: bfloat16 [128, 2, 262144], P('grp', None, 'tpl'), may hold values from -5 to 5
- weights: float32 [3, 262144], P(None, 'tpl'), may hold values from 0.3 to 3
- detectors: int32 [512], P('grp'), may hold values from 0 to 2
- offsets: int32 [512, 4], P('grp'), may hold values from 0 to 1048448
- routes: int32 [512, 4], P('grp'), may hold values from 0 to 31, all different within a row; in each aligned block of 16 rows (0 to 15, 16 to 31, ...) at most 3 rows name the same one
Outputs:
- snr: float32 [512, 4, 4, 128], P('grp', None, None, 'tpl')
- peak: float32 [512, 4, 4], P('grp')
Inputs may be any that keep to these rules, and one draw needn't show every extreme that they name: `routes`: each segment names 4 different groups. Among the 16 segments of one index of grp (aligned blocks) no group is named more than 3 times; in some blocks a group is named exactly 3 times. Every group is named somewhere.
All inputs are finite; a program needn't handle non-finite values.
Results may differ from a plain program's by a relative error of at most 0.0031.
Values may be sent and summed in bfloat16 or wider, within the bound.
A program may use at most 128 MiB of HBM per device.

v0:
```python
import math

import jax
import jax.numpy as jnp
from jax import lax
from jax.sharding import PartitionSpec as P

SAMPLES = 1048576
BLOCK = 256
WINDOW = 128


TWO_PI = 2.0 * math.pi
EPSILON = 1e-06


def turn_angles(freq_index, time_index, samples):
    turned = freq_index * time_index % samples
    return turned.astype(jnp.float32) * (TWO_PI / samples)


def dft_halves(block_len, window, samples):
    inside = jnp.arange(block_len, dtype=jnp.int32)[:, None]
    moment = jnp.arange(window, dtype=jnp.int32)[None, :]
    angles = turn_angles(inside, moment, samples)
    cosine = jnp.cos(angles).astype(jnp.bfloat16)
    sine_part = jnp.sin(angles).astype(jnp.bfloat16)
    upper = jnp.concatenate([cosine, sine_part], axis=1)
    lower = jnp.concatenate([-sine_part, cosine], axis=1)
    return (upper, lower)


def twiddles(first_block, block_count, block_len, window, samples):
    starts = (first_block + jnp.arange(block_count, dtype=jnp.int32)) * block_len
    moment = jnp.arange(window, dtype=jnp.int32)
    angles = turn_angles(starts[:, None], moment[None, :], samples)
    return (jnp.cos(angles), jnp.sin(angles))


def shift_rows(strain, detectors, offsets, weights, first_bin, samples):
    bins_local = strain.shape[-1]
    det_pick = (
        detectors[:, None] == jnp.arange(weights.shape[0], dtype=jnp.int32)[None, :]
    ).astype(jnp.float32)
    weight_rows = jnp.dot(det_pick, weights, precision=lax.Precision.HIGHEST)
    seg_real = strain[:, 0].astype(jnp.float32) * weight_rows
    seg_imag = strain[:, 1].astype(jnp.float32) * weight_rows
    freq_index = first_bin + jnp.arange(bins_local, dtype=jnp.int32)
    angles = turn_angles(freq_index[None, None, :], offsets[:, :, None], samples)
    cosine = jnp.cos(angles)
    sine_part = jnp.sin(angles)
    real_out = seg_real[:, None] * cosine - seg_imag[:, None] * sine_part
    imag_out = seg_real[:, None] * sine_part + seg_imag[:, None] * cosine
    return jnp.stack([real_out, imag_out], axis=2).astype(jnp.bfloat16)


def filter_rows(rows_in, bank_in, upper, lower, twid_cos, twid_sin, block_len):
    seg_real = rows_in[:, None, 0].astype(jnp.float32)
    seg_imag = rows_in[:, None, 1].astype(jnp.float32)
    bank_real = bank_in[:, :, 0].astype(jnp.float32)
    bank_imag = bank_in[:, :, 1].astype(jnp.float32)
    prod_real = (seg_real * bank_real + seg_imag * bank_imag).astype(jnp.bfloat16)
    prod_imag = (seg_imag * bank_real - seg_real * bank_imag).astype(jnp.bfloat16)
    row_total, per_group, bins_local = prod_real.shape
    block_count = bins_local // block_len
    flat_real = prod_real.reshape(-1, block_len)
    flat_imag = prod_imag.reshape(-1, block_len)
    mixed = jnp.dot(flat_real, upper, preferred_element_type=jnp.float32)
    mixed = mixed + jnp.dot(flat_imag, lower, preferred_element_type=jnp.float32)
    window = upper.shape[1] // 2
    mixed = mixed.reshape(row_total, per_group, block_count, 2 * window)
    inner_real = mixed[..., :window]
    inner_imag = mixed[..., window:]
    out_real = jnp.sum(inner_real * twid_cos - inner_imag * twid_sin, axis=2)
    out_imag = jnp.sum(inner_real * twid_sin + inner_imag * twid_cos, axis=2)
    return jnp.stack([out_real, out_imag], axis=2)


def run_blocks(rows_in, bank_in, upper, lower, twid_cos, twid_sin, block_len):
    row_total = rows_in.shape[0]
    step_rows = math.gcd(row_total, 8)
    grouped = rows_in.reshape(row_total // step_rows, step_rows, 2, rows_in.shape[-1])

    def filter_block(rows_part):
        return filter_rows(rows_part, bank_in, upper, lower, twid_cos, twid_sin, block_len)

    outcome = lax.map(filter_block, grouped)
    return outcome.reshape((row_total,) + outcome.shape[2:])


def combine_bins(partial_series):
    whole_sum = lax.psum(partial_series, "tpl")
    magnitude = jnp.sqrt(whole_sum[:, :, 0] ** 2 + whole_sum[:, :, 1] ** 2)
    width_local = magnitude.shape[-1] // lax.axis_size("tpl")
    own_slice = lax.dynamic_slice_in_dim(
        magnitude, lax.axis_index("tpl") * width_local, width_local, 2
    )
    return (own_slice, jnp.max(magnitude, axis=-1))


def body(strain, templates, weights, detectors, offsets, routes):
    seg_rows, triggers = routes.shape
    bins_local = strain.shape[-1]
    groups = lax.axis_size("grp")
    per_group = templates.shape[0]
    first_bin = lax.axis_index("tpl") * bins_local
    block_count = bins_local // BLOCK
    upper, lower = dft_halves(BLOCK, WINDOW, SAMPLES)
    twid_cos, twid_sin = twiddles(
        lax.axis_index("tpl") * block_count, block_count, BLOCK, WINDOW, SAMPLES
    )
    shifted = shift_rows(strain, detectors, offsets, weights, first_bin, SAMPLES)
    shifted = shifted.reshape(seg_rows * triggers, 2, bins_local)
    flat_routes = routes.reshape(-1)
    weight_square = weights * weights
    own_power = templates[:, 0].astype(jnp.float32) ** 2 + templates[:, 1].astype(jnp.float32) ** 2
    own_norm = jnp.dot(own_power, weight_square.T, precision=lax.Precision.HIGHEST)
    partial_norm = lax.all_gather(own_norm, "grp", axis=0, tiled=True)
    capacity = max(2, (3 * seg_rows * triggers + 2 * groups - 1) // (2 * groups))
    slot_total = groups * capacity
    row_total = seg_rows * triggers
    onehot = (flat_routes[:, None] == jnp.arange(groups, dtype=jnp.int32)[None, :]).astype(
        jnp.int32
    )
    slot_rank = jnp.sum((jnp.cumsum(onehot, axis=0) - 1) * onehot, axis=1)
    position = flat_routes * capacity + slot_rank
    slot_match = position[None, :] == jnp.arange(slot_total, dtype=jnp.int32)[:, None]
    source = jnp.sum(
        slot_match.astype(jnp.int32) * jnp.arange(row_total, dtype=jnp.int32)[None, :], axis=1
    )
    filled = jnp.any(slot_match, axis=1)
    outgoing = jnp.where(
        filled[:, None, None], jnp.take(shifted, source, axis=0), jnp.zeros((), jnp.bfloat16)
    )
    outgoing = outgoing.reshape(groups, capacity, 2, bins_local)
    arrived = lax.all_to_all(outgoing, "grp", split_axis=0, concat_axis=0, tiled=True)
    items = arrived.shape[1]
    partial_series = run_blocks(
        arrived.reshape(groups * items, 2, bins_local),
        templates[None],
        upper,
        lower,
        twid_cos,
        twid_sin,
        BLOCK,
    )
    slot_mag, slot_peak = combine_bins(partial_series)
    slot_mag = slot_mag.reshape(groups, items, per_group, slot_mag.shape[-1])
    slot_peak = slot_peak.reshape(groups, items, per_group)
    back_mag = lax.all_to_all(slot_mag, "grp", split_axis=0, concat_axis=0, tiled=True)
    back_peak = lax.all_to_all(slot_peak, "grp", split_axis=0, concat_axis=0, tiled=True)
    magnitude = jnp.take(
        back_mag.reshape(slot_total, per_group, back_mag.shape[-1]), position, axis=0
    )
    peaks = jnp.take(back_peak.reshape(slot_total, per_group), position, axis=0)
    norm_table = lax.psum(partial_norm, "tpl")
    chosen = jnp.take(norm_table.reshape(groups, per_group, weights.shape[0]), flat_routes, axis=0)
    detector_rows = jnp.repeat(detectors, triggers)
    det_pick = (
        detector_rows[:, None] == jnp.arange(weights.shape[0], dtype=jnp.int32)[None, :]
    ).astype(jnp.float32)
    root_norm = jnp.sqrt(jnp.sum(chosen * det_pick[:, None, :], axis=-1) + EPSILON)
    snr = (magnitude / root_norm[..., None]).reshape(
        seg_rows, triggers, per_group, magnitude.shape[-1]
    )
    peak = (peaks / root_norm).reshape(seg_rows, triggers, per_group)
    return (snr, peak)


def solution(mesh):
    return jax.shard_map(
        body,
        mesh=mesh,
        in_specs=(
            P("grp", None, "tpl"),
            P("grp", None, "tpl"),
            P(None, "tpl"),
            P("grp"),
            P("grp", None),
            P("grp", None),
        ),
        out_specs=(P("grp", None, None, "tpl"), P("grp", None, None)),
        check_vma=False,
    )
```

profile of v0, /device:TPU:1, one launch (start us, length us, event | category | flops | bytes accessed | tf_op | source)
XLA Modules:
  0.0 929.1 jit_solution(12365833124261861609)
XLA Ops:
  8.7 5.7 fusion.40
  14.5 4.7 convert_multiply_fusion.1
  19.2 7.0 mul.346
  26.1 10.0 %mul.347 = f32[64,1,32768]{2,0,1:T(8,128)} reshape(f32[16,4,32768]{2,1,0:T(4,128)} %mul.346) | data formatting | bytes 16777216 | tf_op jit(solution)/shard_map/mul | solution.py:52
  36.1 5.4 mul.357
  41.5 10.0 %mul.358 = f32[64,1,32768]{2,0,1:T(8,128)} reshape(f32[16,4,32768]{2,1,0:T(4,128)} %mul.357) | data formatting | bytes 16777216 | tf_op jit(solution)/shard_map/mul | solution.py:52
  51.7 38.0 %subtract_convert_fusion.1 = (bf16[64,1,32768]{2,0,1:T(8,128)(2,1)S(1)}, bf16[64,1,32768]{2,0,1:T(8,128)(2,1)}) fusion(f32[64,1,32768]{2,0,1:T(8,128)} %mul.358, f32[64,1,32768]{2,0,1:T(8,128)} %mul.347, s32[64]{0:T(128)S(1)} %mul.350, s32[32768]{0:T(1024)S(1)} %iota_add_fusion), kind=kLoop, calls=%fused_computation.45 | loop fusion | flops 46137344 | bytes 25297152 | tf_op jit(solution)/shard_map/convert.6
  89.7 6.2 pad_maximum_fusion
  95.8 16.3 %copy.76 = bf16[64,2,32768]{2,1,0:T(2,128)(2,1)} copy(bf16[64,2,32768]{2,0,1:T(8,128)(2,1)} %pad_maximum_fusion) | data formatting | bytes 16777216 | tf_op jit(solution)/shard_map/stack | solution.py:54
  112.3 30.7 %gather_fusion = bf16[96,2,32768]{2,1,0:T(2,128)(2,1)} fusion(bf16[64,2,32768]{2,1,0:T(2,128)(2,1)} %copy.76, s32[1024]{0:T(1024)S(1)} %pad_clamp_fusion.2), kind=kCustom, calls=%fused_computation | custom fusion | bytes 25166208 | tf_op jit(solution)/shard_map/jit(_take)/gather | solution.py:133
  142.9 16.6 %broadcast_select_fusion.1 = bf16[32,3,2,32768]{3,2,1,0:T(2,128)(2,1)} fusion(pred[32,3]{1,0:T(8,128)(4,1)S(1)} %broadcast_in_dim.93, bf16[32,3,2,32768]{3,2,1,0:T(2,128)(2,1)} %bitcast.84, pred[32,3]{1,0:T(8,128)(4,1)S(1)} %compare_and_fusion), kind=kLoop, calls=%fused_computation.34 | loop fusion | flops 12582912 | bytes 25166016 | tf_op jit(solution)/shard_map/jit(_where)/select_n | solution.py:132
  159.6 12.3 %all-to-all-start = ((bf16[32,3,2,32768]{3,2,1,0:T(2,128)(2,1)}), bf16[32,3,2,32768]{3,2,1,0:T(2,128)(2,1)}, u32[]{:S(2)}, u32[]{:S(2)}) async-start(bf16[32,3,2,32768]{3,2,1,0:T(2,128)(2,1)} %broadcast_select_fusion.1), calls=%async_computation | async-start | bytes 25165824 | tf_op jit(solution)/shard_map/all_to_all | solution.py:136
  175.5 328.7 %all-gather = f32[32,4,3]{2,1,0:T(4,128)S(1)} all-gather(f32[1,4,3]{2,1,0:T(4,128)S(1)} %convolution_bitcast_fusion), channel_id=1, replica_groups=mesh['grp'=32,'tpl'=8] {'grp'}, dimensions={0}, use_global_device_ids=true | all-gather | bytes 1584 | tf_op jit(solution)/shard_map/all_gather | solution.py:118
  504.2 31.8 %psum.15 = f32[32,4,3]{2,1,0:T(4,128)S(1)} all-reduce(f32[32,4,3]{2,1,0:T(4,128)S(1)} %all-gather), channel_id=1, replica_groups=mesh['grp'=32,'tpl'=8] {'tpl'}, use_global_device_ids=true, to_apply=%region_9.10 | all-reduce | flops 384 | bytes 3072 | tf_op jit(solution)/shard_map/psum | solution.py:156
  538.4 281.1 %while.12 = (s32[]{:T(128)}, f32[12,8,4,2,128]{4,3,2,1,0:T(2,128)S(1)}, bf16[12,8,2,32768]{3,2,1,0:T(2,128)(2,1)}, bf16[1,4,2,32768]{3,2,1,0:T(2,128)(2,1)S(1)},...) while((s32[]{:T(128)}, ...), condition=%wide.region_7.8_spmd.clone.clone, body=%wide.region_4.7_spmd.clone.clone.sunk | while | flops 1088389120 | bytes 50430556 | solution.py:87
  544.9 3.6 subtract_convert_fusion.3
  568.3 3.6 subtract_convert_fusion.3
  591.7 3.6 subtract_convert_fusion.3
  615.1 3.6 subtract_convert_fusion.3
  638.5 3.6 subtract_convert_fusion.3
  661.9 3.6 subtract_convert_fusion.3
  685.3 3.6 subtract_convert_fusion.3
  708.7 3.6 subtract_convert_fusion.3
  732.1 3.6 subtract_convert_fusion.3
  755.5 3.6 subtract_convert_fusion.3
  778.9 3.6 subtract_convert_fusion.3
  802.4 3.6 subtract_convert_fusion.3
  820.3 64.7 %all-reduce.2.cloned.1.call-done = f32[96,4,2,128]{3,2,1,0:T(2,128)} async-done(((f32[96,4,2,128]{3,2,1,0:T(2,128)}), f32[96,4,2,128]{3,2,1,0:T(2,128)}) %all-reduce.2.cloned.1.call-update) | async-done | bytes 393232 | tf_op jit(solution)/shard_map/psum | solution.py:92
  888.4 9.6 %all-to-all-start.2 = ((f32[32,3,4]{1,2,0:T(4,128)}), f32[32,3,4]{1,2,0:T(4,128)S(1)}, u32[]{:S(2)}, u32[]{:S(2)}) async-start(f32[32,3,4]{1,2,0:T(4,128)} %copy.82), calls=%async_computation.2 | async-start | bytes 131072 | tf_op jit(solution)/shard_map/all_to_all | solution.py:151
  899.2 7.6 all-to-all-done.2
  906.8 3.9 all-to-all-start.1
  912.5 6.8 all-to-all-done.1
  (212 shorter events, 254.1 us)
Async XLA Ops:
  8.7 5.7 copy-start.1
  8.7 5.7 copy-start.3
  41.5 10.0 %copy-start.4 = (s32[16,4]{0,1:T(4,128)S(1)}, s32[16,4]{0,1:T(4,128)}, u32[]{:S(2)}) copy-start(s32[16,4]{0,1:T(4,128)} %param.12) | copy-start | bytes 772
  159.6 12.7 %copy-start = (bf16[4,2,32768]{2,1,0:T(2,128)(2,1)S(1)}, bf16[4,2,32768]{2,1,0:T(2,128)(2,1)}, u32[]{:S(2)}) copy-start(bf16[4,2,32768]{2,1,0:T(2,128)(2,1)} %param.9) | copy-start | bytes 1572868
  159.6 378.8 %all-to-all-start = ((bf16[32,3,2,32768]{3,2,1,0:T(2,128)(2,1)}), bf16[32,3,2,32768]{3,2,1,0:T(2,128)(2,1)}, u32[]{:S(2)}, u32[]{:S(2)}) async-start(bf16[32,3,2,32768]{3,2,1,0:T(2,128)(2,1)} %broadcast_select_fusion.1), calls=%async_computation | async-start | bytes 25165824 | tf_op jit(solution)/shard_map/all_to_all | solution.py:136
  171.9 713.1 %all-reduce.2.cloned.1.call-start = ((), (), s32[]{:S(2)}) async-start(), calls=%async_computation.3 | async-start | bytes 786432 | tf_op jit(solution)/shard_map/psum | solution.py:92
  819.5 0.7 copy-start.2
  888.4 18.4 %all-to-all-start.2 = ((f32[32,3,4]{1,2,0:T(4,128)}), f32[32,3,4]{1,2,0:T(4,128)S(1)}, u32[]{:S(2)}, u32[]{:S(2)}) async-start(f32[32,3,4]{1,2,0:T(4,128)} %copy.82), calls=%async_computation.2 | async-start | bytes 131072 | tf_op jit(solution)/shard_map/all_to_all | solution.py:151
  906.8 12.6 %all-to-all-start.1 = ((f32[32,1,192]{2,1,0:T(1,128)}), f32[32,1,192]{2,1,0:T(1,128)S(1)}, u32[]{:S(2)}, u32[]{:S(2)}) async-start(f32[32,1,192]{2,1,0:T(1,128)} %reshape.444), calls=%async_computation.1 | async-start | bytes 65536 | tf_op jit(solution)/shard_map/all_to_all | solution.py:150
Sparse Core Ops, SparseCore 0:
  820.4 64.5 all-reduce.1
where the time goes:
time: 935 us; the launch traced here: 929 us
  blocking collectives  360 us (39%)
  local copies, waits for them, and re-layouts  217 us (23%)
  other arithmetic  157 us (17%)
  waiting for transfers between devices  79.2 us (8%)
  matrix products  73.7 us (8%)
  starting transfers between devices  25.8 us (3%)
  between operations  14.3 us (2%)
    all_gather x1, blocking collectives, body(): partial_norm = lax.all_gather(own_norm, 'grp', axis=0, tiled=True)  329 us
    psum x1, waiting for transfers between devices, combine_bins(): whole_sum = lax.psum(partial_series, 'tpl')  64.7 us
    convert_element_type x12, other arithmetic, filter_rows(): (seg_imag * bank_real - seg_real * bank_imag).astype(jnp.bfloat16)  43.5 us
    convert_element_type x12, local copies, waits for them, and re-layouts, filter_rows(): (seg_real * bank_real + seg_imag * bank_imag).astype(jnp.bfloat16)  38.8 us
    convert_element_type x12, local copies, waits for them, and re-layouts, filter_rows(): (seg_imag * bank_real - seg_real * bank_imag).astype(jnp.bfloat16)  38.8 us
    another operation x1, other arithmetic  38 us
    dot_general x12, matrix products, filter_rows(): jnp.dot(flat_imag, lower, preferred_element_type=jnp.float32)  34.7 us
    mul x4, local copies, waits for them, and re-layouts, shift_rows(): real_out = seg_real[:, None] * cosine - seg_imag[:, None] * sine_part  32.3 us
  transfers between devices with their start and end apart: 4, of which 3 were waited for; matrix products, arithmetic and copies ran while one was open for 1% of the time, Pallas kernels for 0%

commit v1 on v0

v1 whole, which is shorter than its diff:
```python
import functools
import math

import jax
import jax.numpy as jnp
from jax import lax
from jax.experimental import pallas as pl
from jax.experimental.pallas import tpu as pltpu
from jax.sharding import Mesh
from jax.sharding import PartitionSpec as P

SAMPLES = 1048576
WINDOW = 128
CHUNK = 256
TWO_PI = 2.0 * math.pi
EPSILON = 1e-06


def turns(index, moment):
    angles = (index * moment % SAMPLES).astype(jnp.float32) * (TWO_PI / SAMPLES)
    return jnp.cos(angles), jnp.sin(angles)


def filter_kernel(
    seg_ref, bank_ref, wgt_ref, det_ref, pick_ref, base_ref, step_ref, inner_ref, outer_ref,
    acc_ref, norm_ref, phase_ref,
):
    chunk = pl.program_id(0)

    @pl.when(chunk == 0)
    def _():
        phase_ref[...] = base_ref[...]
        acc_ref[...] = jnp.zeros_like(acc_ref)
        norm_ref[...] = jnp.zeros_like(norm_ref)

    det = det_ref[...]
    wgt = wgt_ref[...]
    chosen = jnp.where(det == 0, wgt[0:1], jnp.where(det == 1, wgt[1:2], wgt[2:3]))
    seg_re = seg_ref[0].astype(jnp.float32) * chosen
    seg_im = seg_ref[1].astype(jnp.float32) * chosen
    rows, width = phase_ref.shape[1], phase_ref.shape[2]
    segs = seg_re.shape[0]
    per = rows // segs
    cos_p = phase_ref[0]
    sin_p = phase_ref[1]
    cos_k = cos_p.reshape(per, segs, width)
    sin_k = sin_p.reshape(per, segs, width)
    sh_re = (seg_re[None] * cos_k - seg_im[None] * sin_k).astype(jnp.bfloat16)
    sh_im = (seg_re[None] * sin_k + seg_im[None] * cos_k).astype(jnp.bfloat16)
    sh_re = sh_re.astype(jnp.float32).reshape(rows, width)
    sh_im = sh_im.astype(jnp.float32).reshape(rows, width)
    cos_s = step_ref[0]
    sin_s = step_ref[1]
    phase_ref[0] = cos_p * cos_s - sin_p * sin_s
    phase_ref[1] = cos_p * sin_s + sin_p * cos_s

    cos_b = outer_ref[0, 0]
    sin_b = outer_ref[0, 1]
    cos_a = inner_ref[0]
    sin_a = inner_ref[1]
    cos_e = (cos_a * cos_b - sin_a * sin_b).astype(jnp.bfloat16)
    sin_e = (sin_a * cos_b + cos_a * sin_b).astype(jnp.bfloat16)
    upper = jnp.concatenate([cos_e, sin_e], axis=1)
    lower = jnp.concatenate([-sin_e, cos_e], axis=1)

    bank_re = bank_ref[0]
    bank_im = bank_ref[1]
    for m in range(acc_ref.shape[0] // rows):
        span = slice(m * rows, (m + 1) * rows)
        pick = pick_ref[span]
        got_re = jnp.dot(pick, bank_re, preferred_element_type=jnp.float32)
        got_im = jnp.dot(pick, bank_im, preferred_element_type=jnp.float32)
        prod_re = (sh_re * got_re + sh_im * got_im).astype(jnp.bfloat16)
        prod_im = (sh_im * got_re - sh_re * got_im).astype(jnp.bfloat16)
        acc_ref[span] += jnp.dot(
            prod_re, upper, preferred_element_type=jnp.float32
        ) + jnp.dot(prod_im, lower, preferred_element_type=jnp.float32)

    power = bank_re.astype(jnp.float32) ** 2 + bank_im.astype(jnp.float32) ** 2
    for d in range(norm_ref.shape[0]):
        scaled = power * (wgt[d : d + 1] * wgt[d : d + 1])
        norm_ref[d] += scaled[:, :128] + scaled[:, 128:]


def filter_bins(seg, bank, wgt, det, pick, base, step, inner, outer):
    bins = seg.shape[-1]
    chunks = bins // CHUNK
    whole = lambda shape: pl.BlockSpec(shape, lambda c: (0,) * len(shape))
    along = lambda shape: pl.BlockSpec(shape, lambda c: (0,) * (len(shape) - 1) + (c,))
    total = pick.shape[0]
    flops = 2 * total * bins * (256 + 512)
    return pl.pallas_call(
        filter_kernel,
        grid=(chunks,),
        in_specs=[
            along((2, seg.shape[1], CHUNK)),
            along((2, bank.shape[1], CHUNK)),
            along((wgt.shape[0], CHUNK)),
            whole(det.shape),
            whole(pick.shape),
            whole(base.shape),
            whole(step.shape),
            whole(inner.shape),
            pl.BlockSpec((1, 2, 1, WINDOW), lambda c: (c, 0, 0, 0)),
        ],
        out_specs=[
            whole((total, 2 * WINDOW)),
            whole((wgt.shape[0], bank.shape[1], 128)),
        ],
        out_shape=[
            jax.ShapeDtypeStruct((total, 2 * WINDOW), jnp.float32),
            jax.ShapeDtypeStruct((wgt.shape[0], bank.shape[1], 128), jnp.float32),
        ],
        scratch_shapes=[pltpu.VMEM(base.shape, jnp.float32)],
        compiler_params=pltpu.CompilerParams(vmem_limit_bytes=48 * 1024 * 1024),
        cost_estimate=pl.CostEstimate(flops=flops, bytes_accessed=8 << 20, transcendentals=0),
    )(seg, bank, wgt, det, pick, base, step, inner, outer)


def body(strain, templates, weights, detectors, offsets, routes):
    home_segs, triggers = routes.shape
    per_group = templates.shape[0]
    ny = lax.axis_size("y")
    nz = lax.axis_size("z")
    bins = strain.shape[-1] // ny
    y = lax.axis_index("y")
    first = (lax.axis_index("x") * lax.axis_size("core") + lax.axis_index("core")) * strain.shape[-1] + y * bins

    seg = lax.all_to_all(strain, "y", split_axis=2, concat_axis=0, tiled=True)
    seg = seg.transpose(1, 0, 2)
    bank = lax.all_to_all(templates, "y", split_axis=2, concat_axis=0, tiled=True)
    bank = lax.all_gather(bank, "z", axis=0, tiled=False)
    bank = bank.reshape(nz, ny, per_group, 2, bins).transpose(3, 1, 0, 2, 4).reshape(2, -1, bins)
    wgt = lax.dynamic_slice_in_dim(weights, y * bins, bins, 1)
    det = lax.all_gather(detectors, "y", axis=0, tiled=True)
    off = lax.all_gather(offsets, "y", axis=0, tiled=True)
    rts = lax.all_gather(routes, "y", axis=0, tiled=True)
    segs = det.shape[0]
    rows = segs * triggers
    off_rows = off.T.reshape(rows, 1)
    rts_rows = rts.T.reshape(rows)

    lanes = jnp.arange(CHUNK, dtype=jnp.int32)
    base = jnp.stack(turns(off_rows, first + lanes[None, :]))
    step = jnp.stack(turns(off_rows, jnp.full((1, CHUNK), CHUNK, jnp.int32)))
    moment = jnp.arange(WINDOW, dtype=jnp.int32)
    inner = jnp.stack(turns(lanes[:, None], moment[None, :]))
    starts = first + CHUNK * jnp.arange(bins // CHUNK, dtype=jnp.int32)
    outer = jnp.stack(turns(starts[:, None], moment[None, :]), axis=1)[:, :, None, :]
    names = (rts_rows[None, :] * per_group + jnp.arange(per_group, dtype=jnp.int32)[:, None]).reshape(-1, 1)
    pick = (names == jnp.arange(bank.shape[1], dtype=jnp.int32)[None, :]).astype(jnp.bfloat16)

    acc, norm = filter_bins(seg, bank, wgt, det[:, None], pick, base, step, inner, outer)

    acc = acc.reshape(per_group * triggers, ny, home_segs * 2 * WINDOW)
    own = lax.psum_scatter(acc, "y", scatter_dimension=1, tiled=False)
    own = lax.psum(own, ("x", "core")).reshape(per_group, triggers, home_segs, 2 * WINDOW)
    norm = lax.psum(jnp.sum(norm, axis=-1), ("y", "x", "core"))
    magnitude = jnp.sqrt(own[..., :WINDOW] ** 2 + own[..., WINDOW:] ** 2)
    magnitude = magnitude.transpose(2, 1, 0, 3)
    peak = jnp.max(magnitude, axis=-1)
    part = lax.axis_size("x") * lax.axis_size("core")
    width = WINDOW // part
    at = lax.axis_index("x") * lax.axis_size("core") + lax.axis_index("core")
    mine = lax.dynamic_slice_in_dim(magnitude, at * width, width, 3)
    table = norm.reshape(norm.shape[0], -1, per_group)
    det_pick = (detectors[:, None] == jnp.arange(norm.shape[0], dtype=jnp.int32)).astype(jnp.float32)
    grp_pick = (routes[:, :, None] == jnp.arange(table.shape[1], dtype=jnp.int32)).astype(jnp.float32)
    by_det = jnp.sum(det_pick[:, :, None, None] * table[None], axis=1)
    power = jnp.sum(grp_pick[..., None] * by_det[:, None], axis=2)
    root = jnp.sqrt(power + EPSILON)
    return mine / root[..., None], peak / root


def solution(mesh):
    ny = 4
    devices = mesh.devices
    nz = devices.shape[0] // ny
    fine = Mesh(devices.reshape(ny, nz, devices.shape[1] // 2, 2), ("y", "z", "x", "core"))
    grp, tpl = ("y", "z"), ("x", "core")
    return jax.shard_map(
        body,
        mesh=fine,
        in_specs=(
            P(grp, None, tpl),
            P(grp, None, tpl),
            P(None, tpl),
            P(grp),
            P(grp, None),
            P(grp, None),
        ),
        out_specs=(P(grp, None, None, tpl), P(grp, None, None)),
        check_vma=False,
    )
```

time: 935 us -> 575 us (0.61)
  blocking collectives: 360 us -> 181 us
  other arithmetic: 157 us -> 7.46 us
  matrix products: 73.7 us -> 0 us
  local copies, waits for them, and re-layouts: 217 us -> 259 us
  Pallas kernels: 0 us -> 37.4 us
  starting transfers between devices: 25.8 us -> 3.87 us
  waiting for transfers between devices: 79.2 us -> 65.8 us
    all_gather x1 -> x2, blocking collectives: 329 us -> 16.1 us  [the longest x1 8.08 us: body(): off = lax.all_gather(offsets, 'y', axis=0, tiled=True)]
    unnamed x15 -> x41, local copies, waits for them, and re-layouts: 3.22 us -> 173 us
    psum x1, blocking collectives: 31.8 us -> 126 us  [body(): norm = lax.psum(jnp.sum(norm, axis=-1), ('y', 'x', 'core'))]
    convert_element_type x24 -> x0, local copies, waits for them, and re-layouts: 77.6 us -> none  [the longest x12 38.8 us: filter_rows(): (seg_real * bank_real + seg_imag * bank_imag).astype(jnp.bfloat16)]
    dot_general x26 -> x0, matrix products: 73.7 us -> none  [the longest x12 34.7 us: filter_rows(): jnp.dot(flat_imag, lower, preferred_element_type=jnp.float32)]
    all_to_all x1 -> x2, local copies, waits for them, and re-layouts: 0.51 us -> 63.5 us  [the longest x1 32.8 us: body(): lax.all_to_all(templates, 'y', split_axis=2, concat_axis=0, tiled=True)]
    convert_element_type x27 -> x4, other arithmetic: 52.9 us -> 1.05 us  [the longest x1 0.89 us: body(): (names == jnp.arange(bank.shape[1], dtype=jnp.int32)[None, :]).astype(jnp...]
    another operation x3, other arithmetic: 44.2 us -> 1.53 us  [the longest x1 0.87 us: body(): base = jnp.stack(turns(off_rows, first + lanes[None, :]))]
  transfers between devices with their start and end apart: 4 -> 4, of which waited for: 3 -> 1; matrix products, arithmetic and copies ran while one was open for 1% -> 17% of each run, Pallas kernels for 0% -> 0%
where the time goes in v1:
time: 575 us; the launch traced here: 569 us
  local copies, waits for them, and re-layouts  259 us (45%)
  blocking collectives  181 us (31%)
  waiting for transfers between devices  65.8 us (11%)
  Pallas kernels  37.4 us (7%)
  between operations  14.6 us (3%)
  other arithmetic  7.46 us (1%)
    unnamed x41, local copies, waits for them, and re-layouts  173 us
    psum x1, blocking collectives, body(): norm = lax.psum(jnp.sum(norm, axis=-1), ('y', 'x', 'core'))  126 us
    psum x1, waiting for transfers between devices, body(): lax.psum(own, ('x', 'core'))  65.7 us
    pallas_call x1, Pallas kernels, filter_bins(): pl.pallas_call(filter_kernel, grid=(chunks,), in_specs=[along((2, seg.sha...  37.4 us
    all_to_all x1, local copies, waits for them, and re-layouts, body(): lax.all_to_all(templates, 'y', split_axis=2, concat_axis=0, tiled=True)  32.8 us
    all_to_all x1, local copies, waits for them, and re-layouts, body(): seg = lax.all_to_all(strain, 'y', split_axis=2, concat_axis=0, tiled=True)  30.7 us
    unnamed x1, blocking collectives  25.3 us
    all_to_all x1, blocking collectives, body(): lax.all_to_all(templates, 'y', split_axis=2, concat_axis=0, tiled=True)  13.4 us
  transfers between devices with their start and end apart: 4, of which 1 were waited for; matrix products, arithmetic and copies ran while one was open for 17% of the time, Pallas kernels for 0%

profile of v1, /device:TPU:1, one launch (start us, length us, event | category | flops | bytes accessed | tf_op | source)
XLA Modules:
  0.0 569.1 jit_solution(7660908791758126708)
XLA Ops:
  7.2 30.2 %copy.68 = bf16[4,2,32768]{0,1,2:T(2,128)(2,1)} copy(bf16[4,2,32768]{2,1,0:T(2,128)(2,1)} %param.7) | data formatting | bytes 1048576 | tf_op args[1]
  37.5 36.7 %reshape.530 = bf16[4,2,32768]{2,1,0:T(2,128)(2,1)S(1)} reshape(bf16[32768,2,4]{2,1,0:T(2,128)(2,1)} %bitcast.46) | data formatting | bytes 1048576
  74.2 13.4 %all_to_all.33 = bf16[4,2,32768]{2,1,0:T(2,128)(2,1)S(1)} all-to-all(bf16[4,2,32768]{2,1,0:T(2,128)(2,1)S(1)} %reshape.530), channel_id=1, replica_groups=mesh['y'=4,'z'=8,'x'=4,'core'=2] {'y'}, dimensions={0} | all-to-all | bytes 1048576 | tf_op jit(solution)/shard_map/all_to_all | solution.py:131
  87.6 37.9 %reshape.531 = bf16[32768,2,4]{2,1,0:T(2,128)(2,1)} reshape(bf16[4,2,32768]{2,1,0:T(2,128)(2,1)S(1)} %all_to_all.33) | data formatting | bytes 1048576
  125.5 32.8 %copy.69 = bf16[4,2,4,8192]{3,1,0,2:T(2,128)(2,1)S(1)} copy(bf16[4,2,4,8192]{0,1,3,2:T(2,128)(2,1)} %bitcast.45) | data formatting | bytes 1048576 | tf_op jit(solution)/shard_map/all_to_all | solution.py:131
  158.3 1.1 copy.70
  159.5 25.4 %copy.66 = bf16[16,2,32768]{0,1,2:T(2,128)(2,1)} copy(bf16[16,2,32768]{2,1,0:T(2,128)(2,1)S(1)} %copy-done.9) | data formatting | bytes 4194304 | tf_op args[0]
  184.8 20.4 %reshape.528 = bf16[4,2,131072]{2,1,0:T(2,128)(2,1)} reshape(bf16[32768,2,16]{2,1,0:T(2,128)(2,1)} %bitcast.44) | data formatting | bytes 4194304
  205.2 3.8 all-to-all-start
  210.6 25.3 %all-reduce = s32[64]{0:T(128)S(1)} all-reduce(s32[64]{0:T(128)S(1)} %dynamic-update-slice), channel_id=1, replica_groups=mesh['y'=4,'z'=8,'x'=4,'core'=2] {'y'}, use_global_device_ids=true, to_apply=%add | all-reduce | flops 64 | bytes 512
  236.6 8.1 %all-gather = s32[4,16,4]{1,2,0:T(4,128)S(1)} all-gather(s32[1,16,4]{1,2,0:T(4,128)S(1)} %bitcast.53), channel_id=1, replica_groups=mesh['y'=4,'z'=8,'x'=4,'core'=2] {'y'}, dimensions={0}, use_global_device_ids=true | all-gather | bytes 1280 | tf_op jit(solution)/shard_map/all_gather | solution.py:137
  244.8 8.1 %all-gather.1 = s32[4,16,4]{1,2,0:T(4,128)S(1)} all-gather(s32[1,16,4]{1,2,0:T(4,128)S(1)} %bitcast.56), channel_id=1, replica_groups=mesh['y'=4,'z'=8,'x'=4,'core'=2] {'y'}, dimensions={0}, use_global_device_ids=true | all-gather | bytes 1280 | tf_op jit(solution)/shard_map/all_gather | solution.py:136
  254.2 1.1 fusion.14
  256.5 0.9 pad_maximum_fusion
  257.4 0.9 fusion.pick_ref
  258.3 13.7 %reshape.529 = bf16[32768,2,16]{2,1,0:T(2,128)(2,1)} reshape(bf16[4,2,131072]{2,1,0:T(2,128)(2,1)S(1)} %all-to-all-done) | data formatting | bytes 4194304
  272.0 30.7 %copy.67 = bf16[16,2,4,8192]{3,0,2,1:T(8,128)(2,1)S(1)} copy(bf16[16,2,4,8192]{0,1,3,2:T(2,128)(2,1)} %bitcast.43) | data formatting | bytes 4194304 | tf_op jit(solution)/shard_map/all_to_all | solution.py:129
  302.8 4.5 copy.71
  307.3 5.3 copy.72
  312.5 6.9 %reshape.513.bank_ref = bf16[2,128,8192]{2,1,0:T(8,128)(2,1)} reshape(bf16[2,4,8,4,8192]{4,3,2,1,0:T(4,128)(2,1)} %copy.72) | data formatting | bytes 8388608 | tf_op jit(solution)/shard_map/reshape | solution.py:133
  319.4 1.0 copy-done.3
  320.5 0.9 copy-done.4
  321.4 0.8 copy-done.7
  322.2 0.8 copy-done.8
  323.0 37.4 %shard_map.77 = (f32[1024,256]{1,0:T(8,128)S(1)}, f32[3,128,128]{2,1,0:T(8,128)S(1)}) custom-call(bf16[2,64,8192]{2,1,0:T(8,128)(2,1)S(1)} %bitcast.41, bf16[2,128,8192]{2,1,0:T(8,128)(2,1)} %reshape.513.bank_ref, f32[3,8192]{1,0:T(4,128)S(1)} %constant_dynamic-slice_fusion.wgt_ref, s32[64,1]{1,0:T(8,128)S(1)} %copy-done.7, bf16[1024,128]{1,0:T(8,128)(2,1)S(1)} %copy-done.4, ...), custom_call_target="tpu_custom_call" | custom-call | flops 12884901888 | bytes 8388608 | tf_op jit(solution)/shard_map/pallas_call | solution.py:92
  360.4 1.0 copy-done.2
  362.0 1.8 reshape.514
  363.8 1.6 copy.77
  365.8 126.3 %psum.15 = f32[3,32,4]{2,1,0:T(8,128)S(1)} all-reduce(f32[3,32,4]{2,1,0:T(8,128)S(1)} %mul.258), channel_id=1, replica_groups=mesh['y'=4,'z'=8,'x'=4,'core'=2] {'y','x','core'}, use_global_device_ids=true, to_apply=%region_3.4 | all-reduce | flops 384 | bytes 3072 | tf_op jit(solution)/shard_map/psum | solution.py:158
  492.2 1.8 copy.83
  494.2 65.7 %all-reduce.3.cloned.1.call-done = f32[4,4,16,256]{3,2,1,0:T(8,128)} async-done(((f32[4,4,16,256]{3,2,1,0:T(8,128)}), f32[4,4,16,256]{3,2,1,0:T(8,128)}) %all-reduce.3.cloned.1.call-update) | async-done | bytes 262160 | tf_op jit(solution)/shard_map/psum | solution.py:157
  559.9 1.1 fusion.26
  (67 shorter events, 7.3 us)
Async XLA Ops:
  7.2 251.1 %copy-start = (f32[3,32768]{1,0:T(4,128)S(1)}, f32[3,32768]{1,0:T(4,128)}, u32[]{:S(2)}) copy-start(f32[3,32768]{1,0:T(4,128)} %param.8) | copy-start | bytes 1179652
  7.2 295.6 %all-gather.4.cloned.1.call-start = ((), (), s32[]{:S(2)}) async-start(), calls=%async_computation.3 | async-start | bytes 4718592 | tf_op jit(solution)/shard_map/all_gather | solution.py:132
  125.5 34.0 %copy-start.9 = (bf16[16,2,32768]{2,1,0:T(2,128)(2,1)S(1)}, bf16[16,2,32768]{2,1,0:T(2,128)(2,1)}, u32[]{:S(2)}) copy-start(bf16[16,2,32768]{2,1,0:T(2,128)(2,1)} %param.6) | copy-start | bytes 6291460
  205.2 3.8 copy-start.13
  205.2 5.1 copy-start.12
  205.2 31.3 %copy-start.10 = (s32[16,4]{0,1:T(4,128)S(1)}, s32[16,4]{0,1:T(4,128)}, u32[]{:S(2)}) copy-start(s32[16,4]{0,1:T(4,128)} %param.11) | copy-start | bytes 772
  205.2 39.6 %copy-start.11 = (s32[16,4]{0,1:T(4,128)S(1)}, s32[16,4]{0,1:T(4,128)}, u32[]{:S(2)}) copy-start(s32[16,4]{0,1:T(4,128)} %param.10) | copy-start | bytes 772
  205.2 53.1 %all-to-all-start = ((bf16[4,2,131072]{2,1,0:T(2,128)(2,1)}), bf16[4,2,131072]{2,1,0:T(2,128)(2,1)S(1)}, u32[]{:S(2)}, u32[]{:S(2)}) async-start(bf16[4,2,131072]{2,1,0:T(2,128)(2,1)} %reshape.528), calls=%async_computation | async-start | bytes 4194304 | tf_op jit(solution)/shard_map/all_to_all | solution.py:129
  209.0 283.2 %reduce-scatter.2.cloned.1.call-start = ((), (), s32[]{:S(2)}) async-start(), calls=%async_computation.4 | async-start | bytes 1310720 | tf_op jit(solution)/shard_map/reduce_scatter | solution.py:156
  319.4 1.0 copy-start.3
  320.5 0.9 copy-start.4
  321.4 0.8 copy-start.7
  322.2 0.8 copy-start.8
  323.0 239.6 %copy-start.1 = (f32[3,32768]{1,0:T(4,128)S(1)}, f32[3,32768]{1,0:T(4,128)}, u32[]{:S(2)}) copy-start(f32[3,32768]{1,0:T(4,128)} %param.8) | copy-start | bytes 1179652
  360.4 1.0 copy-start.2
  361.4 0.7 copy-start.5
  362.0 3.5 copy-start.6
  365.4 194.5 %all-reduce.3.cloned.1.call-start = ((), (), s32[]{:S(2)}) async-start(), calls=%async_computation.5 | async-start | bytes 524288 | tf_op jit(solution)/shard_map/psum | solution.py:157
Sparse Core Ops, SparseCore 0:
  159.6 56.9 all-gather.3
  365.5 33.5 reduce-scatter.1
  494.1 65.7 all-reduce.2

commit v2 on v1

v2 whole, which is shorter than its diff:
```python
import functools
import math

import jax
import jax.numpy as jnp
from jax import lax
from jax.experimental import pallas as pl
from jax.experimental.pallas import tpu as pltpu
from jax.sharding import Mesh
from jax.sharding import PartitionSpec as P

SAMPLES = 1048576
WINDOW = 128
LANES = 128
CHUNK = 2 * LANES
LAG = 2
BANK_PARTS = 4
SEG_PARTS = 8
TWO_PI = 2.0 * math.pi
EPSILON = 1e-06
MESH = pl.DeviceIdType.MESH


def turns(index, moment):
    angles = ((index * moment) & (SAMPLES - 1)).astype(jnp.float32) * (TWO_PI / SAMPLES)
    return jnp.cos(angles), jnp.sin(angles)


def iota(shape, dim):
    return lax.broadcasted_iota(jnp.int32, shape, dim)


def filter_kernel(
    dims, strain, bank, meta, wgt, snr, peak,
    stage_b, stage_s, bank_buf, seg_buf, meta_buf, pick, perm, phase, step, inner, outer,
    acc, norm, nsum, r0, n0, r1, n1, mags,
    bank_load, bank_own, seg_load, yb_send, yb_recv, ys_send, ys_recv, meta_send, meta_recv,
    z_send, z_recv, r0_send, r0_recv, r1_send, r1_recv, r2_send, r2_recv,
):
    nx, ny, nz = dims
    x, y, z, core = (lax.axis_index(a) for a in ("x", "y", "z", "core"))
    home, triggers = strain.shape[0], 4
    per_group = bank.shape[0]
    blocks = bank_buf.shape[0]
    chunks = blocks // 2
    segs = home * ny
    rows = segs * triggers
    names = nz * ny * per_group
    pairs = per_group * triggers
    half = pairs // 2
    share = half // nx
    reach = nz // 2
    bins = blocks * LANES
    first = ((x * 2 + core) * ny + y) * bins
    bank_rows = blocks // BANK_PARTS
    seg_rows = blocks // SEG_PARTS
    up, down = lax.rem(z + 1, nz), lax.rem(z + nz - 1, nz)

    def remote(src, dst, send, recv, where):
        return pltpu.make_async_remote_copy(
            src_ref=src, dst_ref=dst, send_sem=send, recv_sem=recv, device_id=where, device_id_type=MESH
        )

    def other_y(shift):
        return lax.rem(y + shift, ny)

    for m in range(per_group):
        pltpu.make_async_copy(bank.at[m], stage_b.at[:, m], bank_load).start()
    for shift in list(range(1, ny)) + [0]:
        span = pl.ds(other_y(shift) * blocks, blocks)

        def load(s, carry, shift=shift, span=span):
            if shift:
                dst = stage_s.at[shift - 1, :, s]
            else:
                dst = seg_buf.at[:, y * home + s]
            pltpu.make_async_copy(strain.at[s, span], dst, seg_load.at[shift]).start()
            return carry

        lax.fori_loop(0, home, load, 0)

    barrier = pltpu.get_barrier_semaphore()
    plane = [(dx, dy) for dx in range(nx) for dy in range(ny) if dx or dy]
    tpl = [(dx, dc) for dx in range(nx) for dc in range(2) if dx or dc]

    def at_plane(dx, dy):
        return {"x": lax.rem(x + dx, nx), "y": lax.rem(y + dy, ny)}

    def at_tpl(dx, dc):
        return {"x": lax.rem(x + dx, nx), "core": lax.rem(core + dc, 2)}

    greeted = [at_plane(dx, dy) for dx, dy in plane]
    greeted += [at_tpl(dx, dc) for dx, dc in tpl if dc]
    greeted += [{"z": up}, {"z": down}]
    for who in greeted:
        pl.semaphore_signal(barrier, inc=1, device_id=who, device_id_type=MESH)

    cos_a, sin_a = turns(iota((CHUNK, WINDOW), 0), iota((CHUNK, WINDOW), 1))
    inner[0] = cos_a
    inner[1] = sin_a
    cos_b, sin_b = turns(first + CHUNK * iota((chunks, WINDOW), 0), iota((chunks, WINDOW), 1))
    outer[0] = cos_b
    outer[1] = sin_b
    wanted = iota((2 * segs, 2 * segs), 0)
    wanted = jnp.where(wanted < segs, 2 * wanted, 2 * (wanted - segs) + 1)
    perm[...] = jnp.where(wanted == iota((2 * segs, 2 * segs), 1), 1.0, 0.0).astype(jnp.bfloat16)
    meta_buf[y] = meta[...]

    pltpu.make_async_copy(stage_b, stage_b, bank_load).wait()
    own_bank = pltpu.make_async_copy(
        stage_b.at[pl.ds(y * blocks, blocks)], bank_buf.at[:, z, pl.ds(y * per_group, per_group)], bank_own
    )
    own_bank.start()
    pl.semaphore_wait(barrier, len(greeted))

    def bank_part(part, shift):
        span = pl.ds(part * bank_rows, bank_rows)
        return remote(
            stage_b.at[pl.ds(other_y(shift) * blocks + part * bank_rows, bank_rows)],
            bank_buf.at[span, z, pl.ds(y * per_group, per_group)],
            yb_send.at[shift - 1], yb_recv.at[part, shift - 1], {"y": other_y(shift)},
        )

    def meta_part(shift):
        return remote(
            meta, meta_buf.at[y], meta_send.at[shift - 1], meta_recv.at[shift - 1], {"y": other_y(shift)}
        )

    def seg_part(part, shift):
        span = pl.ds(part * seg_rows, seg_rows)
        return remote(
            stage_s.at[shift - 1, span], seg_buf.at[span, pl.ds(y * home, home)],
            ys_send.at[shift - 1], ys_recv.at[part, shift - 1], {"y": other_y(shift)},
        )

    for shift in range(1, ny):
        bank_part(0, shift).start()
    for shift in range(1, ny):
        meta_part(shift).start()
    for part in range(1, BANK_PARTS):
        for shift in range(1, ny):
            bank_part(part, shift).start()
    for shift in range(1, ny):
        pltpu.make_async_copy(stage_s.at[shift - 1], stage_s.at[shift - 1], seg_load.at[shift]).wait()

    def send_segs(part, carry):
        for shift in range(1, ny):
            seg_part(part, shift).start()
        return carry

    lax.fori_loop(0, SEG_PARTS, send_segs, 0)
    own_bank.wait()

    def hop(chunk, h, rise):
        origin = lax.rem(z + (nz - h + 1 if rise else h - 1), nz)
        ref = bank_buf.at[pl.ds(2 * chunk, 2), origin]
        way = 0 if rise else 1
        return remote(
            ref, ref, z_send.at[way, h - 1], z_recv.at[way, h - 1, chunk], {"z": up if rise else down}
        )

    def landed(chunk, h, rise):
        origin = lax.rem(z + (nz - h if rise else h), nz)
        ref = bank_buf.at[pl.ds(2 * chunk, 2), origin]
        way = 0 if rise else 1
        remote(
            ref, ref, z_send.at[way, h - 1], z_recv.at[way, h - 1, chunk], {"z": up if rise else down}
        ).wait_recv()

    def when(cond, run):
        if isinstance(cond, bool):
            if cond:
                run()
        else:
            pl.when(cond)(run)

    def both(a, b):
        if isinstance(a, bool):
            return a and b
        return jnp.logical_and(a, b)

    def tick(t):
        def last(chunk=t - LAG * reach):
            def go():
                when(chunk % 2 == 0, lambda: landed(chunk, reach, True))
                when(chunk % 2 == 1, lambda: landed(chunk, reach, False))

            when(both(chunk >= 0, chunk < chunks), go)

        last()
        for h in range(reach, 0, -1):
            chunk = t - LAG * (h - 1)

            def go(chunk=chunk, h=h):
                if h > 1:
                    landed(chunk, h - 1, True)
                    landed(chunk, h - 1, False)
                else:
                    per_part = bank_rows // 2

                    def arrived():
                        for shift in range(1, ny):
                            bank_part(chunk // per_part, shift).wait_recv()

                    when(chunk % per_part == 0, arrived)
                if h < reach:
                    hop(chunk, h, True).start()
                    hop(chunk, h, False).start()
                else:
                    when(chunk % 2 == 0, lambda: hop(chunk, h, True).start())
                    when(chunk % 2 == 1, lambda: hop(chunk, h, False).start())

            when(both(chunk >= 0, chunk < chunks), go)

    def tables_phase(k):
        info = meta_buf[...].reshape(segs, LANES)
        off = info[:, 1 + k : 2 + k]
        cos_p, sin_p = turns(off, first + iota((segs, CHUNK), 1))
        phase[0, k * segs : (k + 1) * segs] = cos_p
        phase[1, k * segs : (k + 1) * segs] = sin_p
        cos_s, sin_s = turns(off, jnp.full((segs, LANES), CHUNK, jnp.int32))
        step[0, k * segs : (k + 1) * segs] = cos_s
        step[1, k * segs : (k + 1) * segs] = sin_s

    def tables_pick(k):
        info = meta_buf[...].reshape(segs, LANES)
        grp = info[:, 5 + k : 6 + k]
        spot = 2 * per_group * (lax.rem(grp, nz) * ny + lax.div(grp, nz))
        spot = jnp.broadcast_to(spot, (segs, 2 * names)) - iota((segs, 2 * names), 1)
        for m in range(per_group):
            to = slice((m * triggers + k) * segs, (m * triggers + k + 1) * segs)
            for part in range(2):
                hit = spot == -(2 * m + part)
                pick[part, to] = jnp.where(hit, 1.0, 0.0).astype(jnp.bfloat16)

    acc[...] = jnp.zeros_like(acc)
    norm[...] = jnp.zeros_like(norm)
    ramp = LAG * reach
    for t in range(ramp):
        tick(t)
        if t == 1:
            for shift in range(1, ny):
                meta_part(shift).wait_recv()
        for k in range(triggers):
            if t == 2 + k % (ramp - 2):
                tables_phase(k)
                tables_pick(k)
    pltpu.make_async_copy(
        seg_buf.at[:, pl.ds(y * home, home)], seg_buf.at[:, pl.ds(y * home, home)], seg_load.at[0]
    ).wait()

    def filter_chunk(c):
        per_part = seg_rows // 2

        def arrived():
            for shift in range(1, ny):
                seg_part(c // per_part, shift).wait_recv()

        pl.when(c % per_part == 0)(arrived)
        seg = jnp.concatenate([seg_buf[2 * c + i].reshape(2 * segs, LANES) for i in range(2)], axis=1)
        got = jnp.concatenate([bank_buf[2 * c + i].reshape(2 * names, LANES) for i in range(2)], axis=1)
        seg = jnp.dot(perm[...], seg, preferred_element_type=jnp.float32)
        w = wgt[:, pl.ds(pl.multiple_of(y * bins + c * CHUNK, CHUNK), CHUNK)]
        det = meta_buf[...].reshape(segs, LANES)[:, 0:1]
        chosen = jnp.where(det == 0, w[0:1], jnp.where(det == 1, w[1:2], w[2:3]))
        seg_re = (seg[:segs] * chosen)[None]
        seg_im = (seg[segs:] * chosen)[None]
        cos_p = phase[0]
        sin_p = phase[1]
        cos_k = cos_p.reshape(triggers, segs, CHUNK)
        sin_k = sin_p.reshape(triggers, segs, CHUNK)
        sh_re = (seg_re * cos_k - seg_im * sin_k).astype(jnp.bfloat16).astype(jnp.float32).reshape(rows, CHUNK)
        sh_im = (seg_re * sin_k + seg_im * cos_k).astype(jnp.bfloat16).astype(jnp.float32).reshape(rows, CHUNK)
        cos_s = jnp.concatenate([step[0], step[0]], axis=1)
        sin_s = jnp.concatenate([step[1], step[1]], axis=1)
        phase[0] = cos_p * cos_s - sin_p * sin_s
        phase[1] = cos_p * sin_s + sin_p * cos_s

        cos_b = outer[0, pl.ds(c, 1)]
        sin_b = outer[1, pl.ds(c, 1)]
        cos_e = (inner[0] * cos_b - inner[1] * sin_b).astype(jnp.bfloat16)
        sin_e = (inner[1] * cos_b + inner[0] * sin_b).astype(jnp.bfloat16)
        upper = jnp.concatenate([cos_e, sin_e], axis=1)
        lower = jnp.concatenate([-sin_e, cos_e], axis=1)
        for m in range(per_group):
            span = slice(m * rows, (m + 1) * rows)
            got_re = jnp.dot(pick[0, span], got, preferred_element_type=jnp.float32)
            got_im = jnp.dot(pick[1, span], got, preferred_element_type=jnp.float32)
            prod_re = (sh_re * got_re + sh_im * got_im).astype(jnp.bfloat16)
            prod_im = (sh_im * got_re - sh_re * got_im).astype(jnp.bfloat16)
            term = jnp.dot(prod_re, upper, preferred_element_type=jnp.float32)
            term = term + jnp.dot(prod_im, lower, preferred_element_type=jnp.float32)
            acc[m * triggers : (m + 1) * triggers] += term.reshape(triggers, segs, 2 * WINDOW)
        power = got.astype(jnp.float32)
        power = power * power
        for d in range(norm.shape[0]):
            scaled = power * (w[d : d + 1] * w[d : d + 1])
            norm[d] += scaled[:, :LANES] + scaled[:, LANES:]

    def advance(t, carry):
        tick(t)
        filter_chunk(t - ramp)
        return carry

    lax.fori_loop(ramp, chunks + ramp, advance, 0)

    mine = pl.ds(core * half, half)
    theirs = pl.ds((1 - core) * half, half)
    core_part = remote(acc.at[theirs], r0, r0_send.at[0], r0_recv.at[0], {"core": 1 - core})
    core_part.start()
    ones = jnp.ones((8, LANES), jnp.float32)
    for d in range(norm.shape[0]):
        line = lax.dot_general(
            ones, norm[d], (((1,), (1,)), ((), ())),
            precision=lax.Precision.HIGHEST, preferred_element_type=jnp.float32,
        )
        nsum[d : d + 1] = line[0:1]
    nsum[norm.shape[0] :] = jnp.zeros((8 - norm.shape[0], 2 * names), jnp.float32)
    core_norm = remote(nsum, n0, r0_send.at[1], r0_recv.at[1], {"core": 1 - core})
    core_norm.start()
    core_part.wait()
    acc[mine] = acc[mine] + r0[...]
    core_norm.wait()
    nsum[...] = nsum[...] + n0[...]

    def plane_part(i, dx, dy):
        who = at_plane(dx, dy)
        return remote(
            acc.at[pl.ds(core * half + who["x"] * share, share), pl.ds(who["y"] * home, home)],
            r1.at[i], r1_send.at[0, i], r1_recv.at[0, i], who,
        )

    def plane_norm(i, dx, dy):
        return remote(nsum, n1.at[i], r1_send.at[1, i], r1_recv.at[1, i], at_plane(dx, dy))

    for i, (dx, dy) in enumerate(plane):
        plane_part(i, dx, dy).start()
    for i, (dx, dy) in enumerate(plane):
        plane_norm(i, dx, dy).start()
    own = pl.ds(core * half + x * share, share)
    total = acc[own, pl.ds(pl.multiple_of(y * home, home), home)]
    for i, (dx, dy) in enumerate(plane):
        plane_part(i, dx, dy).wait_recv()
        total = total + r1[i]
    mags[own] = jnp.sqrt(total[:, :, :WINDOW] ** 2 + total[:, :, WINDOW:] ** 2)

    def tpl_part(i, dx, dc):
        return remote(mags.at[own], mags.at[own], r2_send.at[i], r2_recv.at[i], at_tpl(dx, dc))

    def tpl_landed(i, dx, dc):
        spot = lax.rem(core + dc, 2) * half + lax.rem(x + nx - dx, nx) * share
        ref = mags.at[pl.ds(spot, share)]
        remote(ref, ref, r2_send.at[i], r2_recv.at[i], at_tpl(dx, dc)).wait_recv()

    for i, (dx, dc) in enumerate(tpl):
        tpl_part(i, dx, dc).start()
    table = nsum[...]
    for i, (dx, dy) in enumerate(plane):
        plane_norm(i, dx, dy).wait_recv()
        table = table + n1[i]
    info = meta[...]
    det = info[:, 0:1]
    chosen = jnp.where(det == 0, table[0:1], jnp.where(det == 1, table[1:2], table[2:3]))
    place = lax.shift_right_logical(iota((home, 2 * names), 1), 1)
    roots = {}
    for k in range(triggers):
        grp = info[:, 5 + k : 6 + k]
        spot = per_group * (lax.rem(grp, nz) * ny + lax.div(grp, nz))
        for m in range(per_group):
            value = jnp.sum(jnp.where(place == spot + m, chosen, 0.0), axis=1, keepdims=True)
            roots[m * triggers + k] = jnp.sqrt(value + EPSILON)
    for i, (dx, dc) in enumerate(tpl):
        tpl_landed(i, dx, dc)
    for pair in range(pairs):
        level = mags[pair]
        snr[pair] = level / roots[pair]
        peak[pair] = jnp.max(level, axis=1, keepdims=True) / roots[pair]

    for shift in range(1, ny):
        remote(stage_b.at[pl.ds(0, blocks)], stage_b.at[pl.ds(0, blocks)], yb_send.at[shift - 1],
               yb_recv.at[0, shift - 1], {"y": other_y(shift)}).wait_send()
        meta_part(shift).wait_send()
        remote(stage_s.at[shift - 1], stage_s.at[shift - 1], ys_send.at[shift - 1],
               ys_recv.at[0, shift - 1], {"y": other_y(shift)}).wait_send()
    for way in range(2):
        for h in range(1, reach + 1):
            ref = bank_buf.at[:, 0] if h < reach else bank_buf.at[pl.ds(0, blocks // 2), 0]
            remote(ref, ref, z_send.at[way, h - 1], z_recv.at[way, h - 1, 0], {"z": up}).wait_send()
    for i, (dx, dy) in enumerate(plane):
        plane_part(i, dx, dy).wait_send()
        plane_norm(i, dx, dy).wait_send()
    for i, (dx, dc) in enumerate(tpl):
        tpl_part(i, dx, dc).wait_send()


def filter_bins(dims, strain, bank, meta, wgt):
    nx, ny, nz = dims
    home, whole_blocks = strain.shape[0], strain.shape[1]
    per_group = bank.shape[0]
    blocks = whole_blocks // ny
    chunks = blocks // 2
    segs, triggers = home * ny, 4
    rows = segs * triggers
    names = nz * ny * per_group
    pairs = per_group * triggers
    half = pairs // 2
    share = half // nx
    near = nx * ny - 1
    reach = nz // 2
    dets = wgt.shape[0]
    f32, bf16 = jnp.float32, jnp.bfloat16
    dma = pltpu.SemaphoreType.DMA
    total = rows * per_group
    any_space = pl.BlockSpec(memory_space=pl.ANY)
    vmem = pl.BlockSpec(memory_space=pltpu.VMEM)
    return pl.pallas_call(
        functools.partial(filter_kernel, dims),
        in_specs=[any_space, any_space, vmem, vmem],
        out_specs=[vmem, vmem],
        out_shape=[
            jax.ShapeDtypeStruct((pairs, home, WINDOW), f32),
            jax.ShapeDtypeStruct((pairs, home, 1), f32),
        ],
        scratch_shapes=[
            pltpu.VMEM((whole_blocks, per_group, 2, LANES), bf16),
            pltpu.VMEM((ny - 1, blocks, home, 2, LANES), bf16),
            pltpu.VMEM((blocks, nz, ny * per_group, 2, LANES), bf16),
            pltpu.VMEM((blocks, segs, 2, LANES), bf16),
            pltpu.VMEM((ny, home, LANES), jnp.int32),
            pltpu.VMEM((2, total, 2 * names), bf16),
            pltpu.VMEM((2 * segs, 2 * segs), bf16),
            pltpu.VMEM((2, rows, CHUNK), f32),
            pltpu.VMEM((2, rows, LANES), f32),
            pltpu.VMEM((2, CHUNK, WINDOW), f32),
            pltpu.VMEM((2, chunks, WINDOW), f32),
            pltpu.VMEM((pairs, segs, 2 * WINDOW), f32),
            pltpu.VMEM((dets, 2 * names, LANES), f32),
            pltpu.VMEM((8, 2 * names), f32),
            pltpu.VMEM((half, segs, 2 * WINDOW), f32),
            pltpu.VMEM((8, 2 * names), f32),
            pltpu.VMEM((near, share, home, 2 * WINDOW), f32),
            pltpu.VMEM((near, 8, 2 * names), f32),
            pltpu.VMEM((pairs, home, WINDOW), f32),
            dma, dma, dma((ny,)),
            dma((ny - 1,)), dma((BANK_PARTS, ny - 1)),
            dma((ny - 1,)), dma((SEG_PARTS, ny - 1)),
            dma((ny - 1,)), dma((ny - 1,)),
            dma((2, reach)), dma((2, reach, chunks)),
            dma((2,)), dma((2,)),
            dma((2, near)), dma((2, near)),
            dma((2 * nx - 1,)), dma((2 * nx - 1,)),
        ],
        compiler_params=pltpu.CompilerParams(
            collective_id=0, has_side_effects=True, vmem_limit_bytes=56 * 1024 * 1024
        ),
        cost_estimate=pl.CostEstimate(
            flops=2 * total * blocks * LANES * 1024, bytes_accessed=4 << 20, transcendentals=0
        ),
    )(strain, bank, meta, wgt)


def body(dims, strain, templates, weights, detectors, offsets, routes):
    nx = dims[0]
    home, triggers = routes.shape

    def by_blocks(a):
        return a.reshape(a.shape[0], 2, -1, LANES).transpose(0, 2, 1, 3)

    meta = jnp.concatenate([detectors[:, None], offsets, routes], axis=1)
    meta = jnp.pad(meta, ((0, 0), (0, LANES - meta.shape[1])))
    snr, peak = filter_bins(dims, by_blocks(strain), by_blocks(templates), meta, weights)
    width = WINDOW // (2 * nx)
    at = lax.axis_index("x") * 2 + lax.axis_index("core")
    snr = lax.dynamic_slice_in_dim(snr, at * width, width, 2)
    snr = snr.reshape(-1, triggers, home, width).transpose(2, 1, 0, 3)
    peak = peak.reshape(-1, triggers, home).transpose(2, 1, 0)
    return snr, peak


def solution(mesh):
    devices = mesh.devices
    ny = 4 if devices.shape[0] % 4 == 0 and devices.shape[0] > 8 else 2
    nz = devices.shape[0] // ny
    nx = devices.shape[1] // 2
    fine = Mesh(devices.reshape(ny, nz, nx, 2), ("y", "z", "x", "core"))
    grp, tpl = ("y", "z"), ("x", "core")
    return jax.shard_map(
        functools.partial(body, (nx, ny, nz)),
        mesh=fine,
        in_specs=(
            P(grp, None, tpl),
            P(grp, None, tpl),
            P(None, tpl),
            P(grp),
            P(grp, None),
            P(grp, None),
        ),
        out_specs=(P(grp, None, None, tpl), P(grp, None, None)),
        check_vma=False,
    )
```

time: 575 us -> 115 us (0.20)
  local copies, waits for them, and re-layouts: 259 us -> 5.2 us
  blocking collectives: 181 us -> 0 us
  Pallas kernels: 37.4 us -> 107 us
  waiting for transfers between devices: 65.8 us -> 0 us
  between operations: 14.6 us -> 0.66 us
  other arithmetic: 7.46 us -> 1.09 us
    unnamed x41 -> x4, local copies, waits for them, and re-layouts: 173 us -> 2.86 us
    psum x1 -> x0, blocking collectives: 126 us -> none  [body(): norm = lax.psum(jnp.sum(norm, axis=-1), ('y', 'x', 'core'))]
    pallas_call x1, Pallas kernels: 37.4 us -> 107 us  [filter_bins(): pl.pallas_call(functools.partial(filter_kernel, dims), in_specs=[any_spac...]
    psum x1 -> x0, waiting for transfers between devices: 65.7 us -> none  [body(): lax.psum(own, ('x', 'core'))]
    all_to_all x2 -> x0, local copies, waits for them, and re-layouts: 63.5 us -> none  [the longest x1 32.8 us: body(): lax.all_to_all(templates, 'y', split_axis=2, concat_axis=0, tiled=True)]
    unnamed x1 -> x0, blocking collectives: 25.3 us -> none
    all_gather x2 -> x0, blocking collectives: 16.1 us -> none  [the longest x1 8.08 us: body(): off = lax.all_gather(offsets, 'y', axis=0, tiled=True)]
    all_to_all x1 -> x0, blocking collectives: 13.4 us -> none  [body(): lax.all_to_all(templates, 'y', split_axis=2, concat_axis=0, tiled=True)]
  transfers between devices with their start and end apart: 4 -> 0, of which waited for: 1 -> 0; matrix products, arithmetic and copies ran while one was open for 17% -> 0% of each run, Pallas kernels for 0% -> 0%
where the time goes in v2:
time: 115 us; the launch traced here: 114 us
  Pallas kernels  107 us (93%)
  local copies, waits for them, and re-layouts  5.2 us (5%)
    pallas_call x1, Pallas kernels, filter_bins(): pl.pallas_call(functools.partial(filter_kernel, dims), in_specs=[any_spac...  107 us
    unnamed x4, local copies, waits for them, and re-layouts  2.86 us

profile of v2, /device:TPU:1, one launch (start us, length us, event | category | flops | bytes accessed | tf_op | source)
XLA Modules:
  0.0 114.4 jit_solution(17484901409656646063)
XLA Ops:
  0.6 0.7 copy.12
  1.4 0.8 copy.13
  2.1 0.8 copy.14
  2.9 0.1 pad_add_fusion
  3.0 0.6 pad.4.meta
  3.6 107.5 %shard_map.77 = (f32[16,16,128]{2,1,0:T(8,128)}, f32[16,16,1]{2,1,0:T(8,128)}) custom-call(bf16[16,256,2,128]{3,2,1,0:T(2,128)(2,1)} %bitcast.16, bf16[4,256,2,128]{3,2,1,0:T(2,128)(2,1)} %bitcast.17, s32[16,128]{1,0:T(8,128)} %pad.4.meta, f32[3,32768]{1,0:T(4,128)} %wgt.1), custom_call_target="tpu_custom_call" | custom-call | flops 17179869184 | bytes 4194304 | tf_op jit(solution)/shard_map/pallas_call | solution.py:416
  111.0 1.0 constant_dynamic-slice_fusion
  112.1 0.7 copy.15
  112.8 1.0 reduce
  113.8 0.6 copy.16

commit v3 on v2

--- a/solution.py
+++ b/solution.py
@@ -13,7 +13,9 @@
 WINDOW = 128
 LANES = 128
 CHUNK = 2 * LANES
+PIECE = 2
 LAG = 2
+BURST = 4
 BANK_PARTS = 4
 SEG_PARTS = 8
 TWO_PI = 2.0 * math.pi
@@ -50,6 +52,9 @@
     half = pairs // 2
     share = half // nx
     reach = nz // 2
+    depth = 2 * PIECE
+    pieces = blocks // depth
+    burst = min(BURST, pieces)
     bins = blocks * LANES
     first = ((x * 2 + core) * ny + y) * bins
     bank_rows = blocks // BANK_PARTS
@@ -153,7 +158,7 @@
 
     def hop(chunk, h, rise):
         origin = lax.rem(z + (nz - h + 1 if rise else h - 1), nz)
-        ref = bank_buf.at[pl.ds(2 * chunk, 2), origin]
+        ref = bank_buf.at[pl.ds(depth * chunk, depth), origin]
         way = 0 if rise else 1
         return remote(
             ref, ref, z_send.at[way, h - 1], z_recv.at[way, h - 1, chunk], {"z": up if rise else down}
@@ -161,7 +166,7 @@
 
     def landed(chunk, h, rise):
         origin = lax.rem(z + (nz - h if rise else h), nz)
-        ref = bank_buf.at[pl.ds(2 * chunk, 2), origin]
+        ref = bank_buf.at[pl.ds(depth * chunk, depth), origin]
         way = 0 if rise else 1
         remote(
             ref, ref, z_send.at[way, h - 1], z_recv.at[way, h - 1, chunk], {"z": up if rise else down}
@@ -179,30 +184,32 @@
             return a and b
         return jnp.logical_and(a, b)
 
+    def enter(chunk):
+        per_part = bank_rows // depth
+
+        def arrived():
+            for shift in range(1, ny):
+                bank_part(chunk // per_part, shift).wait_recv()
+
+        when(chunk % per_part == 0, arrived)
+        hop(chunk, 1, True).start()
+        hop(chunk, 1, False).start()
+
     def tick(t):
         def last(chunk=t - LAG * reach):
             def go():
                 when(chunk % 2 == 0, lambda: landed(chunk, reach, True))
                 when(chunk % 2 == 1, lambda: landed(chunk, reach, False))
 
-            when(both(chunk >= 0, chunk < chunks), go)
+            when(both(chunk >= 0, chunk < pieces), go)
 
         last()
-        for h in range(reach, 0, -1):
+        for h in range(reach, 1, -1):
             chunk = t - LAG * (h - 1)
 
             def go(chunk=chunk, h=h):
-                if h > 1:
-                    landed(chunk, h - 1, True)
-                    landed(chunk, h - 1, False)
-                else:
-                    per_part = bank_rows // 2
-
-                    def arrived():
-                        for shift in range(1, ny):
-                            bank_part(chunk // per_part, shift).wait_recv()
-
-                    when(chunk % per_part == 0, arrived)
+                landed(chunk, h - 1, True)
+                landed(chunk, h - 1, False)
                 if h < reach:
                     hop(chunk, h, True).start()
                     hop(chunk, h, False).start()
@@ -210,7 +217,10 @@
                     when(chunk % 2 == 0, lambda: hop(chunk, h, True).start())
                     when(chunk % 2 == 1, lambda: hop(chunk, h, False).start())
 
-            when(both(chunk >= 0, chunk < chunks), go)
+            when(both(chunk >= 0, chunk < pieces), go)
+
+        fresh = t + burst
+        when(fresh < pieces, lambda: enter(fresh))
 
     def tables_phase(k):
         info = meta_buf[...].reshape(segs, LANES)
@@ -235,28 +245,32 @@
 
     acc[...] = jnp.zeros_like(acc)
     norm[...] = jnp.zeros_like(norm)
+    for c in range(burst):
+        enter(c)
     ramp = LAG * reach
     for t in range(ramp):
         tick(t)
-        if t == 1:
+        if t == 0:
             for shift in range(1, ny):
                 meta_part(shift).wait_recv()
         for k in range(triggers):
-            if t == 2 + k % (ramp - 2):
+            if t == 1 + k * (ramp - 1) // triggers:
                 tables_phase(k)
                 tables_pick(k)
     pltpu.make_async_copy(
         seg_buf.at[:, pl.ds(y * home, home)], seg_buf.at[:, pl.ds(y * home, home)], seg_load.at[0]
     ).wait()
 
-    def filter_chunk(c):
-        per_part = seg_rows // 2
+    def wait_segs(piece):
+        per_part = seg_rows // depth
 
         def arrived():
             for shift in range(1, ny):
-                seg_part(c // per_part, shift).wait_recv()
-
-        pl.when(c % per_part == 0)(arrived)
+                seg_part(piece // per_part, shift).wait_recv()
+
+        pl.when(piece % per_part == 0)(arrived)
+
+    def filter_chunk(c):
         seg = jnp.concatenate([seg_buf[2 * c + i].reshape(2 * segs, LANES) for i in range(2)], axis=1)
         got = jnp.concatenate([bank_buf[2 * c + i].reshape(2 * names, LANES) for i in range(2)], axis=1)
         seg = jnp.dot(perm[...], seg, preferred_element_type=jnp.float32)
@@ -299,15 +313,33 @@
 
     def advance(t, carry):
         tick(t)
-        filter_chunk(t - ramp)
+        wait_segs(t - ramp)
+        for i in range(PIECE):
+            filter_chunk(PIECE * (t - ramp) + i)
         return carry
 
-    lax.fori_loop(ramp, chunks + ramp, advance, 0)
-
-    mine = pl.ds(core * half, half)
-    theirs = pl.ds((1 - core) * half, half)
-    core_part = remote(acc.at[theirs], r0, r0_send.at[0], r0_recv.at[0], {"core": 1 - core})
-    core_part.start()
+    lax.fori_loop(ramp, pieces + ramp, advance, 0)
+
+    def core_part(dx):
+        spot = lax.rem(x + dx, nx) * share
+        return remote(
+            acc.at[pl.ds((1 - core) * half + spot, share)], r0.at[pl.ds(spot, share)],
+            r0_send.at[dx], r0_recv.at[dx], {"core": 1 - core},
+        )
+
+    def plane_part(i, dx, dy):
+        who = at_plane(dx, dy)
+        return remote(
+            acc.at[pl.ds(core * half + who["x"] * share, share), pl.ds(who["y"] * home, home)],
+            r1.at[i], r1_send.at[0, i], r1_recv.at[0, i], who,
+        )
+
+    def plane_norm(i, dx, dy):
+        return remote(nsum, n1.at[i], r1_send.at[1, i], r1_recv.at[1, i], at_plane(dx, dy))
+
+    far_first = sorted(range(nx), key=lambda dx: -min(dx, nx - dx))
+    for dx in far_first:
+        core_part(dx).start()
     ones = jnp.ones((8, LANES), jnp.float32)
     for d in range(norm.shape[0]):
         line = lax.dot_general(
@@ -316,25 +348,18 @@
         )
         nsum[d : d + 1] = line[0:1]
     nsum[norm.shape[0] :] = jnp.zeros((8 - norm.shape[0], 2 * names), jnp.float32)
-    core_norm = remote(nsum, n0, r0_send.at[1], r0_recv.at[1], {"core": 1 - core})
+    core_norm = remote(nsum, n0, r0_send.at[nx], r0_recv.at[nx], {"core": 1 - core})
     core_norm.start()
-    core_part.wait()
-    acc[mine] = acc[mine] + r0[...]
+    for dx in far_first:
+        core_part(dx).wait_recv()
+        spot = lax.rem(x + dx, nx) * share
+        mine = pl.ds(core * half + spot, share)
+        acc[mine] = acc[mine] + r0[pl.ds(spot, share)]
+        for i, (px, py) in enumerate(plane):
+            if px == dx:
+                plane_part(i, px, py).start()
     core_norm.wait()
     nsum[...] = nsum[...] + n0[...]
-
-    def plane_part(i, dx, dy):
-        who = at_plane(dx, dy)
-        return remote(
-            acc.at[pl.ds(core * half + who["x"] * share, share), pl.ds(who["y"] * home, home)],
-            r1.at[i], r1_send.at[0, i], r1_recv.at[0, i], who,
-        )
-
-    def plane_norm(i, dx, dy):
-        return remote(nsum, n1.at[i], r1_send.at[1, i], r1_recv.at[1, i], at_plane(dx, dy))
-
-    for i, (dx, dy) in enumerate(plane):
-        plane_part(i, dx, dy).start()
     for i, (dx, dy) in enumerate(plane):
         plane_norm(i, dx, dy).start()
     own = pl.ds(core * half + x * share, share)
@@ -386,6 +411,8 @@
         for h in range(1, reach + 1):
             ref = bank_buf.at[:, 0] if h < reach else bank_buf.at[pl.ds(0, blocks // 2), 0]
             remote(ref, ref, z_send.at[way, h - 1], z_recv.at[way, h - 1, 0], {"z": up}).wait_send()
+    for dx in far_first:
+        core_part(dx).wait_send()
     for i, (dx, dy) in enumerate(plane):
         plane_part(i, dx, dy).wait_send()
         plane_norm(i, dx, dy).wait_send()
@@ -445,8 +472,8 @@
             dma((ny - 1,)), dma((BANK_PARTS, ny - 1)),
             dma((ny - 1,)), dma((SEG_PARTS, ny - 1)),
             dma((ny - 1,)), dma((ny - 1,)),
-            dma((2, reach)), dma((2, reach, chunks)),
-            dma((2,)), dma((2,)),
+            dma((2, reach)), dma((2, reach, chunks // PIECE)),
+            dma((nx + 1,)), dma((nx + 1,)),
             dma((2, near)), dma((2, near)),
             dma((2 * nx - 1,)), dma((2 * nx - 1,)),
         ],

time: 115 us -> 94.7 us (0.82)
  Pallas kernels: 107 us -> 87.5 us
    pallas_call x1, Pallas kernels: 107 us -> 87.5 us  [filter_bins(): pl.pallas_call(functools.partial(filter_kernel, dims), in_specs=[any_spac...]
where the time goes in v3:
time: 94.7 us; the launch traced here: 94.5 us
  Pallas kernels  87.5 us (92%)
  local copies, waits for them, and re-layouts  5.2 us (5%)
  other arithmetic  1.09 us (1%)
    pallas_call x1, Pallas kernels, filter_bins(): pl.pallas_call(functools.partial(filter_kernel, dims), in_specs=[any_spac...  87.5 us
    unnamed x4, local copies, waits for them, and re-layouts  2.86 us

profile of v3, /device:TPU:1, one launch (start us, length us, event | category | flops | bytes accessed | tf_op | source)
XLA Modules:
  0.0 94.5 jit_solution(1088582824890070743)
XLA Ops:
  0.6 0.7 copy.12
  1.4 0.8 copy.13
  2.1 0.8 copy.14
  2.9 0.1 pad_add_fusion
  3.0 0.6 pad.4.meta
  3.6 87.5 %shard_map.77 = (f32[16,16,128]{2,1,0:T(8,128)}, f32[16,16,1]{2,1,0:T(8,128)}) custom-call(bf16[16,256,2,128]{3,2,1,0:T(2,128)(2,1)} %bitcast.16, bf16[4,256,2,128]{3,2,1,0:T(2,128)(2,1)} %bitcast.17, s32[16,128]{1,0:T(8,128)} %pad.4.meta, f32[3,32768]{1,0:T(4,128)} %wgt.1), custom_call_target="tpu_custom_call" | custom-call | flops 17179869184 | bytes 4194304 | tf_op jit(solution)/shard_map/pallas_call | solution.py:443
  91.1 1.0 %constant_dynamic-slice_fusion = f32[16,16,16]{2,1,0:T(8,128)S(1)} fusion(f32[16,16,128]{2,1,0:T(8,128)} %get-tuple-element.4, s32[]{:T(128)S(6)} %select_n.3), kind=kLoop, calls=%fused_computation.1 | loop fusion | bytes 32772 | tf_op jit(solution)/shard_map/dynamic_slice | solution.py:501
  92.1 0.7 copy.15
  92.8 1.0 %reduce = f32[16,16]{1,0:T(8,128)S(1)} reduce(f32[16,16,1]{2,1,0:T(8,128)} %get-tuple-element.5, f32[]{:T(128)} %constant.23), dimensions={2}, to_apply=%get-tuple-element.5.reduce_sub_computation | reduce | bytes 2052 | tf_op jit(solution)/shard_map/pallas_call | solution.py:443
  93.9 0.6 copy.16

commit v4 on v3

--- a/solution.py
+++ b/solution.py
@@ -33,11 +33,11 @@
 
 
 def filter_kernel(
-    dims, strain, bank, meta, wgt, snr, peak,
-    stage_b, stage_s, bank_buf, seg_buf, meta_buf, pick, perm, phase, step, inner, outer,
-    acc, norm, nsum, r0, n0, r1, n1, mags,
+    dims, strain, bank, dets, offs, names_in, wgt, snr, peak,
+    stage_b, stage_s, bank_buf, seg_buf, meta, meta_buf, pick, perm, phase, step, inner, outer,
+    acc, thin, norm, nsum, n0, r1, n1, mags,
     bank_load, bank_own, seg_load, yb_send, yb_recv, ys_send, ys_recv, meta_send, meta_recv,
-    z_send, z_recv, r0_send, r0_recv, r1_send, r1_recv, r2_send, r2_recv,
+    z_send, z_recv, n0_send, n0_recv, n1_send, n1_recv, r1_send, r1_recv, r2_send, r2_recv,
 ):
     nx, ny, nz = dims
     x, y, z, core = (lax.axis_index(a) for a in ("x", "y", "z", "core"))
@@ -49,8 +49,7 @@
     rows = segs * triggers
     names = nz * ny * per_group
     pairs = per_group * triggers
-    half = pairs // 2
-    share = half // nx
+    share = pairs // (2 * nx)
     reach = nz // 2
     depth = 2 * PIECE
     pieces = blocks // depth
@@ -69,6 +68,23 @@
     def other_y(shift):
         return lax.rem(y + shift, ny)
 
+    barrier = pltpu.get_barrier_semaphore()
+
+    def ring(i, n):
+        return min(i, n - i)
+
+    level = [(dx, dy, dc) for dx in range(nx) for dy in range(ny) for dc in range(2) if dx or dy or dc]
+    level.sort(key=lambda d: -(ring(d[0], nx) + ring(d[1], ny)))
+    plane = [d[:2] for d in level if not d[2]]
+    tpl = [(d[0], d[2]) for d in level if not d[1]]
+
+    def at_level(dx, dy, dc):
+        return {"x": lax.rem(x + dx, nx), "y": lax.rem(y + dy, ny), "core": lax.rem(core + dc, 2)}
+
+    greeted = [at_level(*d) for d in level] + [{"z": up}, {"z": down}]
+    for who in greeted:
+        pl.semaphore_signal(barrier, inc=1, device_id=who, device_id_type=MESH)
+
     for m in range(per_group):
         pltpu.make_async_copy(bank.at[m], stage_b.at[:, m], bank_load).start()
     for shift in list(range(1, ny)) + [0]:
@@ -84,22 +100,49 @@
 
         lax.fori_loop(0, home, load, 0)
 
-    barrier = pltpu.get_barrier_semaphore()
-    plane = [(dx, dy) for dx in range(nx) for dy in range(ny) if dx or dy]
-    tpl = [(dx, dc) for dx in range(nx) for dc in range(2) if dx or dc]
-
-    def at_plane(dx, dy):
-        return {"x": lax.rem(x + dx, nx), "y": lax.rem(y + dy, ny)}
-
-    def at_tpl(dx, dc):
-        return {"x": lax.rem(x + dx, nx), "core": lax.rem(core + dc, 2)}
-
-    greeted = [at_plane(dx, dy) for dx, dy in plane]
-    greeted += [at_tpl(dx, dc) for dx, dc in tpl if dc]
-    greeted += [{"z": up}, {"z": down}]
-    for who in greeted:
-        pl.semaphore_signal(barrier, inc=1, device_id=who, device_id_type=MESH)
-
+    square = (home, home)
+    lines = [dets[...]] + [r[k : k + 1] for r in (offs, names_in) for k in range(triggers)]
+    meta[...] = jnp.zeros_like(meta)
+    for at, line in enumerate(lines):
+        across = jnp.broadcast_to(line.astype(jnp.float32), square)
+        across = jnp.where(iota(square, 0) == iota(square, 1), across, 0.0)
+        meta[:, at : at + 1] = jnp.sum(across, axis=1, keepdims=True).astype(jnp.int32)
+    meta_buf[y] = meta[...]
+
+    pltpu.make_async_copy(stage_b, stage_b, bank_load).wait()
+    own_bank = pltpu.make_async_copy(
+        stage_b.at[pl.ds(y * blocks, blocks)], bank_buf.at[:, z, pl.ds(y * per_group, per_group)], bank_own
+    )
+    own_bank.start()
+    pl.semaphore_wait(barrier, len(greeted))
+
+    def bank_part(part, shift):
+        span = pl.ds(part * bank_rows, bank_rows)
+        return remote(
+            stage_b.at[pl.ds(other_y(shift) * blocks + part * bank_rows, bank_rows)],
+            bank_buf.at[span, z, pl.ds(y * per_group, per_group)],
+            yb_send.at[shift - 1], yb_recv.at[part, shift - 1], {"y": other_y(shift)},
+        )
+
+    def meta_part(shift):
+        return remote(
+            meta, meta_buf.at[y], meta_send.at[shift - 1], meta_recv.at[shift - 1], {"y": other_y(shift)}
+        )
+
+    def seg_part(part, shift):
+        span = pl.ds(part * seg_rows, seg_rows)
+        return remote(
+            stage_s.at[shift - 1, span], seg_buf.at[span, pl.ds(y * home, home)],
+            ys_send.at[shift - 1], ys_recv.at[part, shift - 1], {"y": other_y(shift)},
+        )
+
+    for shift in range(1, ny):
+        bank_part(0, shift).start()
+    for shift in range(1, ny):
+        meta_part(shift).start()
+    for part in range(1, BANK_PARTS):
+        for shift in range(1, ny):
+            bank_part(part, shift).start()
     cos_a, sin_a = turns(iota((CHUNK, WINDOW), 0), iota((CHUNK, WINDOW), 1))
     inner[0] = cos_a
     inner[1] = sin_a
@@ -109,51 +152,8 @@
     wanted = iota((2 * segs, 2 * segs), 0)
     wanted = jnp.where(wanted < segs, 2 * wanted, 2 * (wanted - segs) + 1)
     perm[...] = jnp.where(wanted == iota((2 * segs, 2 * segs), 1), 1.0, 0.0).astype(jnp.bfloat16)
-    meta_buf[y] = meta[...]
-
-    pltpu.make_async_copy(stage_b, stage_b, bank_load).wait()
-    own_bank = pltpu.make_async_copy(
-        stage_b.at[pl.ds(y * blocks, blocks)], bank_buf.at[:, z, pl.ds(y * per_group, per_group)], bank_own
-    )
-    own_bank.start()
-    pl.semaphore_wait(barrier, len(greeted))
-
-    def bank_part(part, shift):
-        span = pl.ds(part * bank_rows, bank_rows)
-        return remote(
-            stage_b.at[pl.ds(other_y(shift) * blocks + part * bank_rows, bank_rows)],
-            bank_buf.at[span, z, pl.ds(y * per_group, per_group)],
-            yb_send.at[shift - 1], yb_recv.at[part, shift - 1], {"y": other_y(shift)},
-        )
-
-    def meta_part(shift):
-        return remote(
-            meta, meta_buf.at[y], meta_send.at[shift - 1], meta_recv.at[shift - 1], {"y": other_y(shift)}
-        )
-
-    def seg_part(part, shift):
-        span = pl.ds(part * seg_rows, seg_rows)
-        return remote(
-            stage_s.at[shift - 1, span], seg_buf.at[span, pl.ds(y * home, home)],
-            ys_send.at[shift - 1], ys_recv.at[part, shift - 1], {"y": other_y(shift)},
-        )
-
-    for shift in range(1, ny):
-        bank_part(0, shift).start()
-    for shift in range(1, ny):
-        meta_part(shift).start()
-    for part in range(1, BANK_PARTS):
-        for shift in range(1, ny):
-            bank_part(part, shift).start()
-    for shift in range(1, ny):
-        pltpu.make_async_copy(stage_s.at[shift - 1], stage_s.at[shift - 1], seg_load.at[shift]).wait()
-
-    def send_segs(part, carry):
-        for shift in range(1, ny):
-            seg_part(part, shift).start()
-        return carry
-
-    lax.fori_loop(0, SEG_PARTS, send_segs, 0)
+    acc[...] = jnp.zeros_like(acc)
+    norm[...] = jnp.zeros_like(norm)
     own_bank.wait()
 
     def hop(chunk, h, rise):
@@ -243,10 +243,17 @@
                 hit = spot == -(2 * m + part)
                 pick[part, to] = jnp.where(hit, 1.0, 0.0).astype(jnp.bfloat16)
 
-    acc[...] = jnp.zeros_like(acc)
-    norm[...] = jnp.zeros_like(norm)
     for c in range(burst):
         enter(c)
+    for shift in range(1, ny):
+        pltpu.make_async_copy(stage_s.at[shift - 1], stage_s.at[shift - 1], seg_load.at[shift]).wait()
+
+    def send_segs(part, carry):
+        for shift in range(1, ny):
+            seg_part(part, shift).start()
+        return carry
+
+    lax.fori_loop(0, SEG_PARTS, send_segs, 0)
     ramp = LAG * reach
     for t in range(ramp):
         tick(t)
@@ -320,62 +327,51 @@
 
     lax.fori_loop(ramp, pieces + ramp, advance, 0)
 
-    def core_part(dx):
-        spot = lax.rem(x + dx, nx) * share
+    def level_part(i):
+        who = at_level(*level[i])
         return remote(
-            acc.at[pl.ds((1 - core) * half + spot, share)], r0.at[pl.ds(spot, share)],
-            r0_send.at[dx], r0_recv.at[dx], {"core": 1 - core},
-        )
-
-    def plane_part(i, dx, dy):
-        who = at_plane(dx, dy)
-        return remote(
-            acc.at[pl.ds(core * half + who["x"] * share, share), pl.ds(who["y"] * home, home)],
-            r1.at[i], r1_send.at[0, i], r1_recv.at[0, i], who,
+            thin.at[pl.ds((who["core"] * nx + who["x"]) * share, share), pl.ds(who["y"] * home, home)],
+            r1.at[i], r1_send.at[i], r1_recv.at[i], who,
         )
 
     def plane_norm(i, dx, dy):
-        return remote(nsum, n1.at[i], r1_send.at[1, i], r1_recv.at[1, i], at_plane(dx, dy))
-
-    far_first = sorted(range(nx), key=lambda dx: -min(dx, nx - dx))
-    for dx in far_first:
-        core_part(dx).start()
+        return remote(nsum, n1.at[i], n1_send.at[i], n1_recv.at[i], at_level(dx, dy, 0))
+
+    thin[...] = acc[...].astype(jnp.bfloat16)
+    for i in range(len(level)):
+        level_part(i).start()
     ones = jnp.ones((8, LANES), jnp.float32)
+    halves = jnp.where(
+        lax.shift_right_logical(iota((2 * names, names), 0), 1) == iota((2 * names, names), 1), 1.0, 0.0
+    )
+    nsum[...] = jnp.zeros_like(nsum)
     for d in range(norm.shape[0]):
         line = lax.dot_general(
             ones, norm[d], (((1,), (1,)), ((), ())),
             precision=lax.Precision.HIGHEST, preferred_element_type=jnp.float32,
         )
+        line = jnp.dot(line, halves, precision=lax.Precision.HIGHEST, preferred_element_type=jnp.float32)
         nsum[d : d + 1] = line[0:1]
-    nsum[norm.shape[0] :] = jnp.zeros((8 - norm.shape[0], 2 * names), jnp.float32)
-    core_norm = remote(nsum, n0, r0_send.at[nx], r0_recv.at[nx], {"core": 1 - core})
+    core_norm = remote(nsum, n0, n0_send, n0_recv, {"core": 1 - core})
     core_norm.start()
-    for dx in far_first:
-        core_part(dx).wait_recv()
-        spot = lax.rem(x + dx, nx) * share
-        mine = pl.ds(core * half + spot, share)
-        acc[mine] = acc[mine] + r0[pl.ds(spot, share)]
-        for i, (px, py) in enumerate(plane):
-            if px == dx:
-                plane_part(i, px, py).start()
     core_norm.wait()
     nsum[...] = nsum[...] + n0[...]
     for i, (dx, dy) in enumerate(plane):
         plane_norm(i, dx, dy).start()
-    own = pl.ds(core * half + x * share, share)
+    own = pl.ds((core * nx + x) * share, share)
     total = acc[own, pl.ds(pl.multiple_of(y * home, home), home)]
-    for i, (dx, dy) in enumerate(plane):
-        plane_part(i, dx, dy).wait_recv()
-        total = total + r1[i]
+    for i in range(len(level)):
+        level_part(i).wait_recv()
+        total = total + r1[i].astype(jnp.float32)
     mags[own] = jnp.sqrt(total[:, :, :WINDOW] ** 2 + total[:, :, WINDOW:] ** 2)
 
     def tpl_part(i, dx, dc):
-        return remote(mags.at[own], mags.at[own], r2_send.at[i], r2_recv.at[i], at_tpl(dx, dc))
+        return remote(mags.at[own], mags.at[own], r2_send.at[i], r2_recv.at[i], at_level(dx, 0, dc))
 
     def tpl_landed(i, dx, dc):
-        spot = lax.rem(core + dc, 2) * half + lax.rem(x + nx - dx, nx) * share
+        spot = (lax.rem(core + dc, 2) * nx + lax.rem(x + nx - dx, nx)) * share
         ref = mags.at[pl.ds(spot, share)]
-        remote(ref, ref, r2_send.at[i], r2_recv.at[i], at_tpl(dx, dc)).wait_recv()
+        remote(ref, ref, r2_send.at[i], r2_recv.at[i], at_level(dx, 0, dc)).wait_recv()
 
     for i, (dx, dc) in enumerate(tpl):
         tpl_part(i, dx, dc).start()
@@ -386,7 +382,7 @@
     info = meta[...]
     det = info[:, 0:1]
     chosen = jnp.where(det == 0, table[0:1], jnp.where(det == 1, table[1:2], table[2:3]))
-    place = lax.shift_right_logical(iota((home, 2 * names), 1), 1)
+    place = iota((home, names), 1)
     roots = {}
     for k in range(triggers):
         grp = info[:, 5 + k : 6 + k]
@@ -396,10 +392,16 @@
             roots[m * triggers + k] = jnp.sqrt(value + EPSILON)
     for i, (dx, dc) in enumerate(tpl):
         tpl_landed(i, dx, dc)
-    for pair in range(pairs):
-        level = mags[pair]
-        snr[pair] = level / roots[pair]
-        peak[pair] = jnp.max(level, axis=1, keepdims=True) / roots[pair]
+    width = snr.shape[-1]
+    turn = lax.rem(WINDOW - (x * 2 + core) * width, WINDOW)
+    tops = jnp.zeros((home, pairs), jnp.float32)
+    for k in range(triggers):
+        for m in range(per_group):
+            ratio = mags[m * triggers + k] / roots[m * triggers + k]
+            top = jnp.max(mags[m * triggers + k], axis=1, keepdims=True) / roots[m * triggers + k]
+            snr[:, k, m, :] = pltpu.roll(ratio, turn, 1)[:, :width]
+            tops = jnp.where(iota((home, pairs), 1) == k * per_group + m, top, tops)
+    peak[...] = tops
 
     for shift in range(1, ny):
         remote(stage_b.at[pl.ds(0, blocks)], stage_b.at[pl.ds(0, blocks)], yb_send.at[shift - 1],
@@ -411,16 +413,15 @@
         for h in range(1, reach + 1):
             ref = bank_buf.at[:, 0] if h < reach else bank_buf.at[pl.ds(0, blocks // 2), 0]
             remote(ref, ref, z_send.at[way, h - 1], z_recv.at[way, h - 1, 0], {"z": up}).wait_send()
-    for dx in far_first:
-        core_part(dx).wait_send()
+    for i in range(len(level)):
+        level_part(i).wait_send()
     for i, (dx, dy) in enumerate(plane):
-        plane_part(i, dx, dy).wait_send()
         plane_norm(i, dx, dy).wait_send()
     for i, (dx, dc) in enumerate(tpl):
         tpl_part(i, dx, dc).wait_send()
 
 
-def filter_bins(dims, strain, bank, meta, wgt):
+def filter_bins(dims, strain, bank, dets, offs, names_in, wgt):
     nx, ny, nz = dims
     home, whole_blocks = strain.shape[0], strain.shape[1]
     per_group = bank.shape[0]
@@ -430,11 +431,11 @@
     rows = segs * triggers
     names = nz * ny * per_group
     pairs = per_group * triggers
-    half = pairs // 2
-    share = half // nx
+    share = pairs // (2 * nx)
     near = nx * ny - 1
+    level = 2 * nx * ny - 1
     reach = nz // 2
-    dets = wgt.shape[0]
+    width = WINDOW // (2 * nx)
     f32, bf16 = jnp.float32, jnp.bfloat16
     dma = pltpu.SemaphoreType.DMA
     total = rows * per_group
@@ -442,17 +443,18 @@
     vmem = pl.BlockSpec(memory_space=pltpu.VMEM)
     return pl.pallas_call(
         functools.partial(filter_kernel, dims),
-        in_specs=[any_space, any_space, vmem, vmem],
+        in_specs=[any_space, any_space, vmem, vmem, vmem, vmem],
         out_specs=[vmem, vmem],
         out_shape=[
-            jax.ShapeDtypeStruct((pairs, home, WINDOW), f32),
-            jax.ShapeDtypeStruct((pairs, home, 1), f32),
+            jax.ShapeDtypeStruct((home, triggers, per_group, width), f32),
+            jax.ShapeDtypeStruct((home, pairs), f32),
         ],
         scratch_shapes=[
             pltpu.VMEM((whole_blocks, per_group, 2, LANES), bf16),
             pltpu.VMEM((ny - 1, blocks, home, 2, LANES), bf16),
             pltpu.VMEM((blocks, nz, ny * per_group, 2, LANES), bf16),
             pltpu.VMEM((blocks, segs, 2, LANES), bf16),
+            pltpu.VMEM((home, LANES), jnp.int32),
             pltpu.VMEM((ny, home, LANES), jnp.int32),
             pltpu.VMEM((2, total, 2 * names), bf16),
             pltpu.VMEM((2 * segs, 2 * segs), bf16),
@@ -461,20 +463,19 @@
             pltpu.VMEM((2, CHUNK, WINDOW), f32),
             pltpu.VMEM((2, chunks, WINDOW), f32),
             pltpu.VMEM((pairs, segs, 2 * WINDOW), f32),
-            pltpu.VMEM((dets, 2 * names, LANES), f32),
-            pltpu.VMEM((8, 2 * names), f32),
-            pltpu.VMEM((half, segs, 2 * WINDOW), f32),
-            pltpu.VMEM((8, 2 * names), f32),
-            pltpu.VMEM((near, share, home, 2 * WINDOW), f32),
-            pltpu.VMEM((near, 8, 2 * names), f32),
+            pltpu.VMEM((pairs, segs, 2 * WINDOW), bf16),
+            pltpu.VMEM((wgt.shape[0], 2 * names, LANES), f32),
+            pltpu.VMEM((8, names), f32),
+            pltpu.VMEM((8, names), f32),
+            pltpu.VMEM((level, share, home, 2 * WINDOW), bf16),
+            pltpu.VMEM((near, 8, names), f32),
             pltpu.VMEM((pairs, home, WINDOW), f32),
             dma, dma, dma((ny,)),
             dma((ny - 1,)), dma((BANK_PARTS, ny - 1)),
             dma((ny - 1,)), dma((SEG_PARTS, ny - 1)),
             dma((ny - 1,)), dma((ny - 1,)),
             dma((2, reach)), dma((2, reach, chunks // PIECE)),
-            dma((nx + 1,)), dma((nx + 1,)),
-            dma((2, near)), dma((2, near)),
+            dma, dma, dma((near,)), dma((near,)), dma((level,)), dma((level,)),
             dma((2 * nx - 1,)), dma((2 * nx - 1,)),
         ],
         compiler_params=pltpu.CompilerParams(
@@ -483,25 +484,19 @@
         cost_estimate=pl.CostEstimate(
             flops=2 * total * blocks * LANES * 1024, bytes_accessed=4 << 20, transcendentals=0
         ),
-    )(strain, bank, meta, wgt)
+    )(strain, bank, dets, offs, names_in, wgt)
 
 
 def body(dims, strain, templates, weights, detectors, offsets, routes):
-    nx = dims[0]
     home, triggers = routes.shape
 
     def by_blocks(a):
         return a.reshape(a.shape[0], 2, -1, LANES).transpose(0, 2, 1, 3)
 
-    meta = jnp.concatenate([detectors[:, None], offsets, routes], axis=1)
-    meta = jnp.pad(meta, ((0, 0), (0, LANES - meta.shape[1])))
-    snr, peak = filter_bins(dims, by_blocks(strain), by_blocks(templates), meta, weights)
-    width = WINDOW // (2 * nx)
-    at = lax.axis_index("x") * 2 + lax.axis_index("core")
-    snr = lax.dynamic_slice_in_dim(snr, at * width, width, 2)
-    snr = snr.reshape(-1, triggers, home, width).transpose(2, 1, 0, 3)
-    peak = peak.reshape(-1, triggers, home).transpose(2, 1, 0)
-    return snr, peak
+    snr, peak = filter_bins(
+        dims, by_blocks(strain), by_blocks(templates), detectors[None, :], offsets.T, routes.T, weights
+    )
+    return snr, peak.reshape(home, triggers, -1)
 
 
 def solution(mesh):

time: 94.7 us -> 87.6 us (0.925)
  Pallas kernels: 87.5 us -> 83.8 us
  local copies, waits for them, and re-layouts: 5.2 us -> 2.93 us
  other arithmetic: 1.09 us -> 0 us
    pallas_call x1, Pallas kernels: 87.5 us -> 83.8 us  [filter_bins(): pl.pallas_call(functools.partial(filter_kernel, dims), in_specs=[any_spac...]
    pallas_call x0 -> x1, local copies, waits for them, and re-layouts: none -> 1.37 us  [filter_bins(): pl.pallas_call(functools.partial(filter_kernel, dims), in_specs=[any_spac...]
    unnamed x4 -> x1, local copies, waits for them, and re-layouts: 2.86 us -> 1.57 us
    pallas_call x1 -> x0, other arithmetic: 1.01 us -> none  [filter_bins(): pl.pallas_call(functools.partial(filter_kernel, dims), in_specs=[any_spac...]
    dynamic_slice x1 -> x0, local copies, waits for them, and re-layouts: 1 us -> none  [body(): snr = lax.dynamic_slice_in_dim(snr, at * width, width, 2)]
where the time goes in v4:
time: 87.6 us; the launch traced here: 87.4 us
  Pallas kernels  83.8 us (96%)
  local copies, waits for them, and re-layouts  2.93 us (3%)
    pallas_call x1, Pallas kernels, filter_bins(): pl.pallas_call(functools.partial(filter_kernel, dims), in_specs=[any_spac...  83.8 us

profile of v4, /device:TPU:1, one launch (start us, length us, event | category | flops | bytes accessed | tf_op | source)
XLA Modules:
  0.0 87.4 jit_solution(2826974434579697599)
XLA Ops:
  0.6 83.8 %shard_map.77 = (f32[16,4,4,16]{3,2,1,0:T(4,128)}, f32[16,16]{1,0:T(8,128)}) custom-call(bf16[16,256,2,128]{3,2,1,0:T(2,128)(2,1)} %bitcast.11, bf16[4,256,2,128]{3,2,1,0:T(2,128)(2,1)} %bitcast.12, s32[1,16]{1,0:T(1,128)} %bitcast.15, s32[4,16]{1,0:T(4,128)} %bitcast.13, s32[4,16]{1,0:T(4,128)} %bitcast.14, f32[3,32768]{1,0:T(4,128)} %wgt.1), custom_call_target="tpu_custom_call" | custom-call | flops 17179869184 | bytes 4194304 | tf_op jit(solution)/shard_map/pallas_call | solution.py:444
  84.5 1.4 %copy.9 = f32[16,16]{0,1:T(8,128)} copy(f32[16,16]{1,0:T(8,128)} %get-tuple-element.5) | data formatting | bytes 2048 | tf_op jit(solution)/shard_map/pallas_call | solution.py:444
  85.9 1.6 %copy.11 = f32[16,4,4,16]{3,2,1,0:T(4,128)} copy(f32[16,4,4,16]{3,2,1,0:T(4,128)} %get-tuple-element.10) | data formatting | bytes 32768

commit v5 on v4

--- a/solution.py
+++ b/solution.py
@@ -15,8 +15,8 @@
 CHUNK = 2 * LANES
 PIECE = 2
 LAG = 2
-BURST = 4
-BANK_PARTS = 4
+BURST = 2
+BANK_PARTS = 8
 SEG_PARTS = 8
 TWO_PI = 2.0 * math.pi
 EPSILON = 1e-06

time: 87.6 us -> 87 us (level)
  no operation moved by 1% of the time
where the time goes in v5:
time: 87 us; the launch traced here: 86.8 us
  Pallas kernels  83.2 us (96%)
  local copies, waits for them, and re-layouts  2.93 us (3%)
    pallas_call x1, Pallas kernels, filter_bins(): pl.pallas_call(functools.partial(filter_kernel, dims), in_specs=[any_spac...  83.2 us

profile of v5, /device:TPU:1, one launch (start us, length us, event | category | flops | bytes accessed | tf_op | source)
XLA Modules:
  0.0 86.8 jit_solution(14462809419652008844)
XLA Ops:
  0.6 83.2 %shard_map.77 = (f32[16,4,4,16]{3,2,1,0:T(4,128)}, f32[16,16]{1,0:T(8,128)}) custom-call(bf16[16,256,2,128]{3,2,1,0:T(2,128)(2,1)} %bitcast.11, bf16[4,256,2,128]{3,2,1,0:T(2,128)(2,1)} %bitcast.12, s32[1,16]{1,0:T(1,128)} %bitcast.15, s32[4,16]{1,0:T(4,128)} %bitcast.13, s32[4,16]{1,0:T(4,128)} %bitcast.14, f32[3,32768]{1,0:T(4,128)} %wgt.1), custom_call_target="tpu_custom_call" | custom-call | flops 17179869184 | bytes 4194304 | tf_op jit(solution)/shard_map/pallas_call | solution.py:444
  83.9 1.4 %copy.9 = f32[16,16]{0,1:T(8,128)} copy(f32[16,16]{1,0:T(8,128)} %get-tuple-element.5) | data formatting | bytes 2048 | tf_op jit(solution)/shard_map/pallas_call | solution.py:444
  85.2 1.6 %copy.11 = f32[16,4,4,16]{3,2,1,0:T(4,128)} copy(f32[16,4,4,16]{3,2,1,0:T(4,128)} %get-tuple-element.10) | data formatting | bytes 32768
